TPU v7x, 256 devices: a whole 4x4x8 slice. The times are simulated.
256 devices in a mesh: tile: 128 (over x, z, y), tm: 2 (over core).
Axes of the slice: x: 4, y: 4, z: 8, core: 2. Of those that a mesh axis runs over, the one named last changes fastest.
Arguments:
- clip_frames: bfloat16 [8, 1024, 6144], P('tm', 'tile'), may hold values from -6 to 6
- first_gain: float32 [96], replicated, may hold values from 0.1 to 1.9
- first_weight: bfloat16 [3, 3, 288, 96], replicated, may hold values from -0.125 to 0.125
- second_gain: float32 [96], replicated, may hold values from 0.1 to 1.9
- second_weight: bfloat16 [3, 3, 288, 96], replicated, may hold values from -0.125 to 0.125
- live_widths: int32 [128], P('tile'), may hold values from 32 to 64, as said below
- band_links: int32 [128, 2], P('tile'), may hold values from 0 to 1, as said below
Outputs:
- encoded: bfloat16 [8, 1024, 6144], P('tm', 'tile')
Inputs may be any that keep to these rules, and one draw needn't show every extreme that they name: `live_widths`: the bands of one video are consecutive; all bands of a video have the same live width, one of 32, 48 and 64, and each of these occurs in every draw. band_links[b,1] equals band_links[b+1,0]; band_links[0,0] and the last band's column 1 are 0.
All inputs are finite; a program needn't handle non-finite values.
Results may differ from a plain program's by a relative error of at most 0.004.
Values may be sent and summed in bfloat16 or wider, within the bound.
No kernel may reach another device: no remote copies, remote signals or barrier semaphores. Data moves between devices by JAX's collectives and lax.ppermute only.
A program may use at most 64 MiB of HBM per device.

v0:
```python
import jax
import jax.numpy as jnp
from jax import lax
from jax.sharding import PartitionSpec as P

C = 96


def shifted(shard, axis, by):
    peers = lax.axis_size(axis)
    pairs = [(i, i + by) for i in range(peers) if 0 <= i + by < peers]
    return lax.ppermute(shard, axis, pairs)


def extended(cells, sides, width):
    for axis, dim in sides:
        count = lax.axis_size(axis)
        ends = count - 1
        head = lax.slice_in_dim(cells, 0, width, axis=dim)
        tail = lax.slice_in_dim(cells, cells.shape[dim] - width, cells.shape[dim], axis=dim)
        cells = jnp.concatenate(
            [
                lax.ppermute(tail, axis, [(i, (i + 1) % count) for i in range(ends)]),
                cells,
                lax.ppermute(head, axis, [((i + 1) % count, i) for i in range(ends)]),
            ],
            axis=dim,
        )
    return cells


def settle(values, gain_vec):
    mean_sq = jnp.mean(values * values, axis=-1, keepdims=True)
    return jax.nn.silu(values * lax.rsqrt(mean_sq + 1e-06) * gain_vec)


def convolve(padded, weight):
    frames_out = padded.shape[0] - 2
    rows_out = padded.shape[1] - 2
    cols_out = padded.shape[2]
    channels = padded.shape[3]
    widened = jnp.pad(padded, ((0, 0), (0, 0), (1, 1), (0, 0)))
    accumulated = jnp.zeros((frames_out * rows_out * cols_out, channels), jnp.float32)
    for tap_t in range(3):
        for tap_h in range(3):
            window_slab = widened[tap_t : tap_t + frames_out, tap_h : tap_h + rows_out]
            tap_cols = jnp.concatenate(
                [window_slab[:, :, tap_w : tap_w + cols_out] for tap_w in range(3)], axis=-1
            )
            accumulated = accumulated + jnp.dot(
                tap_cols.reshape(-1, 3 * channels),
                weight[tap_t, tap_h],
                preferred_element_type=jnp.float32,
            )
    return accumulated.reshape(frames_out, rows_out, cols_out, channels)


def edge_rows(padded, has_above, has_below, depth):
    row_count = padded.shape[1]
    row_index = jnp.arange(row_count)
    row_weight = jnp.where(
        row_index < depth, has_above, jnp.where(row_index >= row_count - depth, has_below, 1.0)
    )
    row_weight = row_weight.reshape((1, row_count) + (1,) * (padded.ndim - 2))
    return padded * row_weight.astype(padded.dtype)


def local(
    clip_frames, first_gain, first_weight, second_gain, second_weight, live_widths, band_links
):
    frames_here, rows_here, wide_here = clip_frames.shape
    cols_here = wide_here // C
    column_mask = (jnp.arange(cols_here) < live_widths[0]).astype(jnp.float32)[:, None]
    has_above = band_links[0, 0].astype(jnp.float32)
    has_below = band_links[0, 1].astype(jnp.float32)
    source = clip_frames.reshape(frames_here, rows_here, cols_here, C).astype(jnp.float32)
    first_hidden = (
        (settle(source, first_gain) * column_mask)
        .astype(jnp.bfloat16)
        .reshape(frames_here, rows_here, wide_here)
    )
    earlier_first = shifted(first_hidden[frames_here - 2 :], "tm", 1)
    joined_first = jnp.concatenate([earlier_first, first_hidden], axis=0)
    padded_first = edge_rows(extended(joined_first, (("tile", 1),), 1), has_above, has_below, 1)
    first_out = convolve(
        padded_first.reshape(frames_here + 2, rows_here + 2, cols_here, C), first_weight
    )
    second_hidden = (
        (settle(first_out, second_gain) * column_mask)
        .astype(jnp.bfloat16)
        .reshape(frames_here, rows_here, wide_here)
    )
    earlier_second = shifted(second_hidden[frames_here - 2 :], "tm", 1)
    joined_second = jnp.concatenate([earlier_second, second_hidden], axis=0)
    padded_second = edge_rows(extended(joined_second, (("tile", 1),), 1), has_above, has_below, 1)
    second_out = convolve(
        padded_second.reshape(frames_here + 2, rows_here + 2, cols_here, C), second_weight
    )
    encoded = ((source + second_out) * column_mask).astype(jnp.bfloat16)
    return encoded.reshape(frames_here, rows_here, wide_here)


def solution(mesh):
    in_specs = (P("tm", "tile", None), P(), P(), P(), P(), P("tile"), P("tile", None))
    out_specs = P("tm", "tile", None)
    return jax.shard_map(local, mesh=mesh, in_specs=in_specs, out_specs=out_specs, check_vma=False)
```

profile of v0, /device:TPU:6, one launch (start us, length us, event | category | flops | bytes accessed | tf_op | source)
XLA Modules:
  0.0 101.6 jit_solution(654027784775216046)
XLA Ops:
  0.0 1.4 %reshape.154 = f32[4,8,64,96]{3,2,1,0:T(8,128)S(1)} reshape(bf16[4,8,6144]{2,1,0:T(8,128)(2,1)} %param.7) | data formatting | bytes 1179648 | tf_op jit(solution)/shard_map/convert_element_type | solution.py:76
  1.5 0.3 multiply_reduce_fusion
  2.5 0.3 fusion.52
  3.4 1.9 %collective-permute-start = (bf16[2,8,6144]{2,1,0:T(8,128)(2,1)S(1)}, bf16[2,8,6144]{2,1,0:T(8,128)(2,1)S(1)}, u32[]{:S(2)}, u32[]{:S(2)}) collective-permute-start(bf16[2,8,6144]{2,1,0:T(8,128)(2,1)S(1)} %slice.337), channel_id=1, source_target_pairs={{0,1},{2,3},{4,5},{6,7},{8,9},{10,11},{12,13},{14,15},{16,17},{18,... | collective-permute-start | bytes 589832 | tf_op jit(solution)/shard_map/ppermute | solution.py:12
  5.6 0.6 mul.137
  6.8 0.6 fusion.55
  9.2 10.5 %collective-permute-start.2 = (bf16[6,1,6144]{2,1,0:T(2,128)(2,1)S(1)}, bf16[6,1,6144]{2,1,0:T(2,128)(2,1)S(1)}, u32[]{:S(2)}, u32[]{:S(2)}) collective-permute-start(bf16[6,1,6144]{2,1,0:T(2,128)(2,1)S(1)} %get-tuple-element.66), channel_id=1, source_target_pairs={{2,0},{4,2},{6,4},{8,6},{10,8},{12,10},{14,12},{16,14},{18,16},{20... | collective-permute-start | bytes 221192 | tf_op jit(solution)/shard_map/ppermute | solution.py:25
  19.7 1.9 %collective-permute-start.1 = (bf16[6,1,6144]{2,1,0:T(2,128)(2,1)S(1)}, bf16[6,1,6144]{2,1,0:T(2,128)(2,1)S(1)}, u32[]{:S(2)}, u32[]{:S(2)}) collective-permute-start(bf16[6,1,6144]{2,1,0:T(2,128)(2,1)S(1)} %get-tuple-element.65), channel_id=1, source_target_pairs={{0,2},{2,4},{4,6},{6,8},{8,10},{10,12},{12,14},{14,16},{16,18},{18... | collective-permute-start | bytes 221192 | tf_op jit(solution)/shard_map/ppermute | solution.py:23
  21.6 0.8 concatenate.82
  22.4 0.4 reduce.2
  23.0 7.9 %collective-permute-done.1 = bf16[6,1,6144]{2,1,0:T(2,128)(2,1)S(1)} collective-permute-done((bf16[6,1,6144]{2,1,0:T(2,128)(2,1)S(1)}, bf16[6,1,6144]{2,1,0:T(2,128)(2,1)S(1)}, u32[]{:S(2)}, u32[]{:S(2)}) %collective-permute-start.1) | collective-permute-done | bytes 73760 | tf_op jit(solution)/shard_map/ppermute | solution.py:23
  30.9 0.4 reduce.1
  31.7 1.5 %pad_slice_fusion.27 = (bf16[4,8,64,96]{3,2,1,0:T(8,128)(2,1)S(1)}, bf16[4,8,64,96]{3,2,1,0:T(8,128)(2,1)S(1)}, bf16[4,8,64,96]{3,2,1,0:T(8,128)(2,1)S(1)}, bf16...) fusion(bf16[6,10,64,96]{3,2,1,0:T(8,128)(2,1)S(1)} %maximum_mul, ...), kind=kLoop, calls=%fused_computation.132 | loop fusion | bytes 5439488 | tf_op jit(solution)/shard_map/slice | solution.py:48
  33.3 0.6 fusion.54
  33.9 2.1 %pad_slice_fusion.26 = (bf16[4,8,64,96]{3,2,1,0:T(8,128)(2,1)S(1)}, bf16[4,8,64,96]{3,2,1,0:T(8,128)(2,1)S(1)}, bf16[4,8,64,96]{3,2,1,0:T(8,128)(2,1)S(1)}, bf16...) fusion(bf16[6,10,64,96]{3,2,1,0:T(8,128)(2,1)S(1)} %maximum_mul, ...), kind=kLoop, calls=%fused_computation.131 | loop fusion | bytes 6881280 | tf_op jit(solution)/shard_map/slice | solution.py:48
  36.0 1.6 %pad_maximum_fusion = (bf16[4,8,64,288]{3,2,1,0:T(8,128)(2,1)S(1)}, bf16[4,8,64,288]{3,2,1,0:T(8,128)(2,1)S(1)}) fusion(bf16[4,8,64,96]{3,2,1,0:T(8,128)(2,1)S(1)} %get-tuple-element.37, bf16[4,8,64,96]{3,2,1,0:T(8,128)(2,1)S(1)} %get-tuple-element.61, bf16[4,8,64,96]{3,2,1,0:T(8,128)(2,1)S(1)} %get-tuple-element.62, ...), kind=kLoop, calls=%fused_computation.16 | loop fusion | flops 7077888 | bytes 4718592 | tf_op jit(solution)/shard_map/concatenate | solution.py:47
  37.6 0.6 fusion.30
  38.2 0.6 convolution_add_fusion.15
  38.8 1.6 %pad_maximum_fusion.2 = (bf16[4,8,64,288]{3,2,1,0:T(8,128)(2,1)S(1)}, bf16[4,8,64,288]{3,2,1,0:T(8,128)(2,1)S(1)}) fusion(bf16[4,8,64,96]{3,2,1,0:T(8,128)(2,1)S(1)} %get-tuple-element.41, bf16[4,8,64,96]{3,2,1,0:T(8,128)(2,1)S(1)} %get-tuple-element.59, bf16[4,8,64,96]{3,2,1,0:T(8,128)(2,1)S(1)} %get-tuple-element.40, ...), kind=kLoop, calls=%fused_computation.18 | loop fusion | flops 7077888 | bytes 4718592 | tf_op jit(solution)/shard_map/concatenate | solution.py:47
  40.4 0.6 convolution_add_fusion.14
  41.0 0.6 convolution_add_fusion.13
  41.7 1.6 %pad_maximum_fusion.4 = (bf16[4,8,64,288]{3,2,1,0:T(8,128)(2,1)S(1)}, bf16[4,8,64,288]{3,2,1,0:T(8,128)(2,1)S(1)}) fusion(bf16[4,8,64,96]{3,2,1,0:T(8,128)(2,1)S(1)} %get-tuple-element.47, bf16[4,8,64,96]{3,2,1,0:T(8,128)(2,1)S(1)} %get-tuple-element.57, bf16[4,8,64,96]{3,2,1,0:T(8,128)(2,1)S(1)} %get-tuple-element.44, ...), kind=kLoop, calls=%fused_computation.20 | loop fusion | flops 7077888 | bytes 4718592 | tf_op jit(solution)/shard_map/concatenate | solution.py:47
  43.3 0.6 convolution_add_fusion.12
  43.9 1.6 %pad_maximum_fusion.5 = (bf16[4,8,64,288]{3,2,1,0:T(8,128)(2,1)S(1)}, bf16[4,8,64,288]{3,2,1,0:T(8,128)(2,1)S(1)}) fusion(bf16[4,8,64,96]{3,2,1,0:T(8,128)(2,1)S(1)} %get-tuple-element.49, bf16[4,8,64,96]{3,2,1,0:T(8,128)(2,1)S(1)} %get-tuple-element.56, bf16[4,8,64,96]{3,2,1,0:T(8,128)(2,1)S(1)} %get-tuple-element.48, ...), kind=kLoop, calls=%fused_computation.21 | loop fusion | flops 7077888 | bytes 4718592 | tf_op jit(solution)/shard_map/concatenate | solution.py:47
  45.5 0.6 convolution_add_fusion.11
  46.1 0.6 convolution_add_fusion.10
  46.7 0.8 pad_maximum_fusion.7
  47.5 0.6 convolution_add_fusion.9
  48.1 0.6 multiply_reduce_fusion.1
  49.1 0.6 reshape.143
  50.2 1.5 %mul.157 = f32[4,8,6144]{2,1,0:T(8,128)} reshape(f32[4,8,64,96]{3,2,1,0:T(8,128)S(1)} %mul.151) | data formatting | bytes 1572864 | tf_op jit(solution)/shard_map/mul | solution.py:34
  51.7 12.3 %fusion.51 = (f32[4,8,64,96]{3,2,1,0:T(8,128)S(1)}, f32[4,8,64,96]{3,2,1,0:T(8,128)S(1)}) fusion(f32[96]{0:T(128)S(1)} %copy-done.6, f32[4,8,64,96]{3,2,1,0:T(8,128)S(1)} %bitcast.109, f32[4,8,64]{2,1,0:T(8,128)S(1)} %rsqrt.21), kind=kLoop, calls=%fused_computation.149 | loop fusion | flops 589824 | bytes 2367872 | tf_op jit(solution)/shard_map/jit(silu)/neg | solution.py:34
  64.5 1.3 %collective-permute-start.3 = (bf16[2,8,6144]{2,1,0:T(8,128)(2,1)S(1)}, bf16[2,8,6144]{2,1,0:T(8,128)(2,1)S(1)}, u32[]{:S(2)}, u32[]{:S(2)}) collective-permute-start(bf16[2,8,6144]{2,1,0:T(8,128)(2,1)S(1)} %slice.379), channel_id=1, source_target_pairs={{0,1},{2,3},{4,5},{6,7},{8,9},{10,11},{12,13},{14,15},{16,17},{18,... | collective-permute-start | bytes 589832 | tf_op jit(solution)/shard_map/ppermute | solution.py:12
  66.1 0.8 collective-permute-done.3
  67.2 1.9 %collective-permute-start.5 = (bf16[6,1,6144]{2,1,0:T(2,128)(2,1)S(1)}, bf16[6,1,6144]{2,1,0:T(2,128)(2,1)S(1)}, u32[]{:S(2)}, u32[]{:S(2)}) collective-permute-start(bf16[6,1,6144]{2,1,0:T(2,128)(2,1)S(1)} %get-tuple-element.64), channel_id=1, source_target_pairs={{2,0},{4,2},{6,4},{8,6},{10,8},{12,10},{14,12},{16,14},{18,16},{20... | collective-permute-start | bytes 221192 | tf_op jit(solution)/shard_map/ppermute | solution.py:25
  69.1 3.9 %collective-permute-start.4 = (bf16[6,1,6144]{2,1,0:T(2,128)(2,1)S(1)}, bf16[6,1,6144]{2,1,0:T(2,128)(2,1)S(1)}, u32[]{:S(2)}, u32[]{:S(2)}) collective-permute-start(bf16[6,1,6144]{2,1,0:T(2,128)(2,1)S(1)} %get-tuple-element.63), channel_id=1, source_target_pairs={{0,2},{2,4},{4,6},{6,8},{8,10},{10,12},{12,14},{14,16},{16,18},{18... | collective-permute-start | bytes 221192 | tf_op jit(solution)/shard_map/ppermute | solution.py:23
  73.1 0.8 concatenate.96
  73.9 1.3 %collective-permute-done.5 = bf16[6,1,6144]{2,1,0:T(2,128)(2,1)S(1)} collective-permute-done((bf16[6,1,6144]{2,1,0:T(2,128)(2,1)S(1)}, bf16[6,1,6144]{2,1,0:T(2,128)(2,1)S(1)}, u32[]{:S(2)}, u32[]{:S(2)}) %collective-permute-start.5) | collective-permute-done | bytes 73760 | tf_op jit(solution)/shard_map/ppermute | solution.py:25
  75.2 0.4 reduce.4
  75.8 5.6 %collective-permute-done.4 = bf16[6,1,6144]{2,1,0:T(2,128)(2,1)S(1)} collective-permute-done((bf16[6,1,6144]{2,1,0:T(2,128)(2,1)S(1)}, bf16[6,1,6144]{2,1,0:T(2,128)(2,1)S(1)}, u32[]{:S(2)}, u32[]{:S(2)}) %collective-permute-start.4) | collective-permute-done | bytes 73760 | tf_op jit(solution)/shard_map/ppermute | solution.py:23
  81.4 0.4 reduce.3
  82.2 1.5 %pad_slice_fusion.9 = (bf16[4,8,64,96]{3,2,1,0:T(8,128)(2,1)S(1)}, bf16[4,8,64,96]{3,2,1,0:T(8,128)(2,1)S(1)}, bf16[4,8,64,96]{3,2,1,0:T(8,128)(2,1)S(1)}, bf16[...) fusion(bf16[6,10,64,96]{3,2,1,0:T(8,128)(2,1)S(1)} %maximum_mul, ...), kind=kLoop, calls=%fused_computation.114 | loop fusion | bytes 5439488 | tf_op jit(solution)/shard_map/slice | solution.py:48
  83.7 0.9 fusion.53
  84.6 2.0 %pad_slice_fusion.8 = (bf16[4,8,64,96]{3,2,1,0:T(8,128)(2,1)S(1)}, bf16[4,8,64,96]{3,2,1,0:T(8,128)(2,1)S(1)}, bf16[4,8,64,96]{3,2,1,0:T(8,128)(2,1)S(1)}, bf16[...) fusion(bf16[6,10,64,96]{3,2,1,0:T(8,128)(2,1)S(1)} %maximum_mul, ...), kind=kLoop, calls=%fused_computation.113 | loop fusion | bytes 6881280 | tf_op jit(solution)/shard_map/slice | solution.py:48
  86.6 0.8 pad_maximum_fusion.9
  87.7 0.6 fusion.20
  88.3 0.8 pad_maximum_fusion.10
  89.1 0.6 convolution_add_fusion.7
  89.7 0.8 pad_maximum_fusion.11
  90.5 0.6 convolution_add_fusion.6
  91.1 0.8 pad_maximum_fusion.12
  91.9 0.6 convolution_add_fusion.5
  92.6 0.8 pad_maximum_fusion.13
  93.4 0.6 convolution_add_fusion.4
  94.0 0.8 pad_maximum_fusion.14
  94.8 0.6 convolution_add_fusion.3
  95.4 0.8 pad_maximum_fusion.15
  96.2 0.6 convolution_add_fusion.2
  96.8 0.8 pad_maximum_fusion.16
  97.6 0.6 convolution_add_fusion.1
  98.2 0.8 pad_maximum_fusion.17
  99.0 0.6 convolution_add_fusion
  100.0 0.6 reshape.153
  100.6 0.8 multiply_convert_fusion
  (47 shorter events, 5.4 us)
Async XLA Ops:
  0.0 2.5 %copy-start.5 = (f32[96]{0:T(128)S(1)}, f32[96]{0:T(128)}, u32[]{:S(2)}) copy-start(f32[96]{0:T(128)} %param.8) | copy-start | bytes 1156
  3.4 3.1 %copy-start = (bf16[4,8,6144]{2,1,0:T(8,128)(2,1)S(1)}, bf16[4,8,6144]{2,1,0:T(8,128)(2,1)}, u32[]{:S(2)}) copy-start(bf16[4,8,6144]{2,1,0:T(8,128)(2,1)} %param.7) | copy-start | bytes 1179652
  3.4 5.4 %collective-permute-start = (bf16[2,8,6144]{2,1,0:T(8,128)(2,1)S(1)}, bf16[2,8,6144]{2,1,0:T(8,128)(2,1)S(1)}, u32[]{:S(2)}, u32[]{:S(2)}) collective-permute-start(bf16[2,8,6144]{2,1,0:T(8,128)(2,1)S(1)} %slice.337), channel_id=1, source_target_pairs={{0,1},{2,3},{4,5},{6,7},{8,9},{10,11},{12,13},{14,15},{16,17},{18,... | collective-permute-start | bytes 589832 | tf_op jit(solution)/shard_map/ppermute | solution.py:12
  5.6 1.2 %copy-start.4 = (s32[1,2]{1,0:T(1,128)S(1)}, s32[1,2]{1,0:T(1,128)}, u32[]{:S(2)}) copy-start(s32[1,2]{1,0:T(1,128)} %param.13) | copy-start | bytes 28
  5.6 3.1 %copy-start.6 = (f32[96]{0:T(128)S(1)}, f32[96]{0:T(128)}, u32[]{:S(2)}) copy-start(f32[96]{0:T(128)} %param.10) | copy-start | bytes 1156
  9.2 13.3 %collective-permute-start.2 = (bf16[6,1,6144]{2,1,0:T(2,128)(2,1)S(1)}, bf16[6,1,6144]{2,1,0:T(2,128)(2,1)S(1)}, u32[]{:S(2)}, u32[]{:S(2)}) collective-permute-start(bf16[6,1,6144]{2,1,0:T(2,128)(2,1)S(1)} %get-tuple-element.66), channel_id=1, source_target_pairs={{2,0},{4,2},{6,4},{8,6},{10,8},{12,10},{14,12},{16,14},{18,16},{20... | collective-permute-start | bytes 221192 | tf_op jit(solution)/shard_map/ppermute | solution.py:25
  19.7 11.3 %collective-permute-start.1 = (bf16[6,1,6144]{2,1,0:T(2,128)(2,1)S(1)}, bf16[6,1,6144]{2,1,0:T(2,128)(2,1)S(1)}, u32[]{:S(2)}, u32[]{:S(2)}) collective-permute-start(bf16[6,1,6144]{2,1,0:T(2,128)(2,1)S(1)} %get-tuple-element.65), channel_id=1, source_target_pairs={{0,2},{2,4},{4,6},{6,8},{8,10},{10,12},{12,14},{14,16},{16,18},{18... | collective-permute-start | bytes 221192 | tf_op jit(solution)/shard_map/ppermute | solution.py:23
  36.0 1.6 %copy-start.2 = (bf16[3,3,288,96]{3,2,1,0:T(8,128)(2,1)S(1)}, bf16[3,3,288,96]{3,2,1,0:T(8,128)(2,1)}, u32[]{:S(2)}) copy-start(bf16[3,3,288,96]{3,2,1,0:T(8,128)(2,1)} %param.9) | copy-start | bytes 1492996
  64.0 1.8 %copy-start.1 = (f32[4,8,6144]{2,1,0:T(8,128)S(1)}, f32[4,8,6144]{2,1,0:T(8,128)}, u32[]{:S(2)}) copy-start(f32[4,8,6144]{2,1,0:T(8,128)} %mul.157) | copy-start | bytes 2359300
  64.5 2.4 %collective-permute-start.3 = (bf16[2,8,6144]{2,1,0:T(8,128)(2,1)S(1)}, bf16[2,8,6144]{2,1,0:T(8,128)(2,1)S(1)}, u32[]{:S(2)}, u32[]{:S(2)}) collective-permute-start(bf16[2,8,6144]{2,1,0:T(8,128)(2,1)S(1)} %slice.379), channel_id=1, source_target_pairs={{0,1},{2,3},{4,5},{6,7},{8,9},{10,11},{12,13},{14,15},{16,17},{18,... | collective-permute-start | bytes 589832 | tf_op jit(solution)/shard_map/ppermute | solution.py:12
  67.2 8.0 %collective-permute-start.5 = (bf16[6,1,6144]{2,1,0:T(2,128)(2,1)S(1)}, bf16[6,1,6144]{2,1,0:T(2,128)(2,1)S(1)}, u32[]{:S(2)}, u32[]{:S(2)}) collective-permute-start(bf16[6,1,6144]{2,1,0:T(2,128)(2,1)S(1)} %get-tuple-element.64), channel_id=1, source_target_pairs={{2,0},{4,2},{6,4},{8,6},{10,8},{12,10},{14,12},{16,14},{18,16},{20... | collective-permute-start | bytes 221192 | tf_op jit(solution)/shard_map/ppermute | solution.py:25
  69.1 12.2 %collective-permute-start.4 = (bf16[6,1,6144]{2,1,0:T(2,128)(2,1)S(1)}, bf16[6,1,6144]{2,1,0:T(2,128)(2,1)S(1)}, u32[]{:S(2)}, u32[]{:S(2)}) collective-permute-start(bf16[6,1,6144]{2,1,0:T(2,128)(2,1)S(1)} %get-tuple-element.63), channel_id=1, source_target_pairs={{0,2},{2,4},{4,6},{6,8},{8,10},{10,12},{12,14},{14,16},{16,18},{18... | collective-permute-start | bytes 221192 | tf_op jit(solution)/shard_map/ppermute | solution.py:23
  86.6 1.1 %copy-start.3 = (bf16[3,3,288,96]{3,2,1,0:T(8,128)(2,1)S(1)}, bf16[3,3,288,96]{3,2,1,0:T(8,128)(2,1)}, u32[]{:S(2)}) copy-start(bf16[3,3,288,96]{3,2,1,0:T(8,128)(2,1)} %param.11) | copy-start | bytes 1492996
where the time goes:
time: 102 us
  other arithmetic  31.8 us (31%)
  starting transfers between devices  21.4 us (21%)
  local copies, waits for them, and re-layouts  18.8 us (18%)
  waiting for transfers between devices  15.6 us (15%)
  matrix products  11.3 us (11%)
  between operations  2.7 us (3%)
    concatenate x14, other arithmetic, convolve(): jnp.concatenate([window_slab[:, :, tap_w:tap_w + cols_out] for tap_w in r...  14.2 us
    ppermute x2, waiting for transfers between devices, extended(): lax.ppermute(tail, axis, [(i, (i + 1) % count) for i in range(ends)])  13.5 us
    neg x2, other arithmetic, settle(): return jax.nn.silu(values * lax.rsqrt(mean_sq + 1e-06) * gain_vec)  12.6 us
    ppermute x2, starting transfers between devices, extended(): lax.ppermute(head, axis, [((i + 1) % count, i) for i in range(ends)])  12.4 us
    dot_general x18, matrix products, convolve(): jnp.dot(tap_cols.reshape(-1, 3 * channels), weight[tap_t, tap_h], preferr...  11.3 us
    slice x6, local copies, waits for them, and re-layouts, convolve(): window_slab[:, :, tap_w:tap_w + cols_out]  8.62 us
    ppermute x2, starting transfers between devices, extended(): lax.ppermute(tail, axis, [(i, (i + 1) % count) for i in range(ends)])  5.86 us
    ppermute x2, starting transfers between devices, shifted(): return lax.ppermute(shard, axis, pairs)  3.18 us
  transfers between devices with their start and end apart: 6, of which 4 were waited for; matrix products, arithmetic and copies ran while one was open for 5% of the time, Pallas kernels for 0%

commit v1 on v0

v1 whole, which is shorter than its diff:
```python
import jax
import jax.numpy as jnp
from jax import lax
from jax.experimental import pallas as pl
from jax.experimental.pallas import tpu as pltpu
from jax.sharding import PartitionSpec as P

C = 96
L = 128
BW = 64
BF = jnp.bfloat16
F32 = jnp.float32
VM = pltpu.VMEM
vmem = pl.BlockSpec(memory_space=pltpu.VMEM)
smem = pl.BlockSpec(memory_space=pltpu.SMEM)
PARAMS = pltpu.CompilerParams(vmem_limit_bytes=32 * 1024 * 1024)


def settle(x, half_gain, mask):
    ms = jnp.sum(x * x, axis=-1, keepdims=True) * (1.0 / C)
    v = x * (lax.rsqrt(ms + 1e-6) * mask) * half_gain
    return v + v * jnp.tanh(v)


def column_mask(widths):
    return (lax.broadcasted_iota(jnp.int32, (BW, 1), 0) < widths[0]).astype(F32)


def half_gain_of(gain):
    g = gain[...] * 0.5
    return jnp.concatenate([g, jnp.zeros((1, L - C), F32)], axis=1)


def spread(frame, scratch):
    pad = jnp.zeros((8, L - C), F32)
    for w in range(BW):
        piece = jnp.concatenate([frame[:, w * C : (w + 1) * C], pad], axis=1)
        scratch[pl.ds(w, 8, stride=BW), :] = piece


def shifts(h):
    row = lax.broadcasted_iota(jnp.int32, (BW, 1), 0)
    left = jnp.where(row == 0, 0.0, pltpu.roll(h, 1, 0))
    right = jnp.where(row == BW - 1, 0.0, pltpu.roll(h, BW - 1, 0))
    return left.astype(BF), h.astype(BF), right.astype(BF)


def put(ref, t, r, h):
    for k, v in enumerate(shifts(h)):
        ref[k, t, r] = v


def pack_weights(weight, packed):
    zero = jnp.zeros((L, L), BF)
    for i in range(3):
        for k in range(3):
            blocks = []
            for j in range(3):
                w = weight[i, j, k * C : (k + 1) * C, :]
                w = jnp.concatenate([w, jnp.zeros((C, L - C), BF)], axis=1)
                blocks.append(jnp.concatenate([w, jnp.zeros((L - C, L), BF)], axis=0))
            for half in range(2):
                for a in range(2):
                    for b in range(2):
                        j = 2 * half + a - b
                        row = (i * 3 + k) * 256 + a * L
                        packed[half, row : row + L, b * L : (b + 1) * L] = blocks[j] if 0 <= j <= 2 else zero


def half_conv(field, frames, row, packed, half):
    pieces = []
    for i in range(3):
        for k in range(3):
            for a in range(2):
                pieces.append(field[k, i : i + frames, row + a].reshape(frames * BW, L))
    return jnp.dot(jnp.concatenate(pieces, axis=1), packed[half], preferred_element_type=F32)


def send_kernel(clip, gain, widths, top, bottom, scratch):
    g = half_gain_of(gain)
    mask = column_mask(widths)
    for t in range(4):
        spread(clip[t].astype(F32), scratch)
        for out, rows in ((top, (0, 1)), (bottom, (6, 7))):
            for n, r in enumerate(rows):
                out[t, n] = settle(scratch[r * BW : (r + 1) * BW, :], g, mask).astype(BF)


def pre_kernel(
    clip, earlier, gain1, weight1, gain2, weight2, widths,
    packed1, packed2, part1, part2, inner, x1, x2, scratch,
):
    mask = column_mask(widths)
    g1, g2 = half_gain_of(gain1), half_gain_of(gain2)
    pack_weights(weight1, packed1)
    pack_weights(weight2, packed2)
    for t in range(8):
        spread((earlier[t] if t < 4 else clip[t - 4]).astype(F32), scratch)
        for r in range(8):
            put(x1, t, r, settle(scratch[r * BW : (r + 1) * BW, :], g1, mask))
    part1[0] = half_conv(x1, 6, 0, packed1, 1)
    part1[1] = half_conv(x1, 6, 6, packed1, 0)
    for p in range(1, 4):
        acc = half_conv(x1, 6, 2 * p - 2, packed1, 0) + half_conv(x1, 6, 2 * p, packed1, 1)
        for t in range(6):
            for b in range(2):
                put(x2, t, 2 * p - 2 + b, settle(acc[t * BW : (t + 1) * BW, b * L : (b + 1) * L], g2, mask))
    part2[0] = half_conv(x2, 4, 0, packed2, 1)
    part2[1] = half_conv(x2, 4, 4, packed2, 0)
    for q in range(1, 3):
        inner[q - 1] = half_conv(x2, 4, 2 * q - 2, packed2, 0) + half_conv(x2, 4, 2 * q, packed2, 1)


def post_kernel(
    clip, up, down, up_early, down_early, gain2, widths, links,
    packed1, packed2, part1, part2, inner, out, x1, x2, scratch,
):
    mask = column_mask(widths)
    g2 = half_gain_of(gain2)
    for side, (now, early) in enumerate(((up, up_early), (down, down_early))):
        link = links[0, side].astype(F32)
        for t in range(8):
            for r in range(2):
                h = (early[t, r] if t < 4 else now[t - 4, r]).astype(F32) * link
                put(x1.at[side], t, r, h)
        acc = part1[side] + half_conv(x1.at[side], 6, 0, packed1, side)
        for t in range(6):
            for b in range(2):
                outer = link if b == side else 1.0
                h = settle(acc[t * BW : (t + 1) * BW, b * L : (b + 1) * L], g2, mask * outer)
                put(x2.at[side], t, b, h)
    outer_rows = [part2[s] + half_conv(x2.at[s], 4, 0, packed2, s) for s in range(2)]
    live = lax.broadcasted_iota(jnp.int32, (8, BW * C), 1) < widths[0] * C
    for t in range(4):
        for q in range(4):
            acc = inner[q - 1] if q in (1, 2) else outer_rows[q // 3]
            for b in range(2):
                r = 2 * q + b
                scratch[r * BW : (r + 1) * BW, :] = acc[t * BW : (t + 1) * BW, b * L : (b + 1) * L]
        pieces = [scratch[pl.ds(w, 8, stride=BW), :][:, :C] for w in range(BW)]
        y = jnp.concatenate(pieces, axis=1)
        out[t] = jnp.where(live, clip[t].astype(F32) + y, 0.0).astype(BF)


def local(clip, gain1, weight1, gain2, weight2, widths, links):
    tiles = lax.axis_size("tile")
    ups = [(i, i + 1) for i in range(tiles - 1)]
    downs = [(i + 1, i) for i in range(tiles - 1)]
    gain1, gain2 = gain1.reshape(1, C), gain2.reshape(1, C)
    edge = VM((4, 2, BW, L), BF)
    top, bottom = pl.pallas_call(
        send_kernel,
        out_shape=(edge, edge),
        in_specs=[vmem, vmem, smem],
        out_specs=(vmem, vmem),
        scratch_shapes=[VM((8 * BW, L), F32)],
        compiler_params=PARAMS,
    )(clip, gain1, widths)
    up = lax.ppermute(bottom, "tile", ups)
    earlier = lax.ppermute(clip, "tm", [(0, 1)])
    down = lax.ppermute(top, "tile", downs)
    packed1, packed2, part1, part2, inner = pl.pallas_call(
        pre_kernel,
        out_shape=(
            VM((2, 9 * 256, 256), BF),
            VM((2, 9 * 256, 256), BF),
            VM((2, 6 * BW, 256), F32),
            VM((2, 4 * BW, 256), F32),
            VM((2, 4 * BW, 256), F32),
        ),
        in_specs=[vmem] * 6 + [smem],
        out_specs=(vmem,) * 5,
        scratch_shapes=[VM((3, 8, 8, BW, L), BF), VM((3, 6, 6, BW, L), BF), VM((8 * BW, L), F32)],
        compiler_params=PARAMS,
    )(clip, earlier, gain1, weight1, gain2, weight2, widths)
    up_early = lax.ppermute(up, "tm", [(0, 1)])
    down_early = lax.ppermute(down, "tm", [(0, 1)])
    return pl.pallas_call(
        post_kernel,
        out_shape=jax.ShapeDtypeStruct((4, 8, BW * C), BF),
        in_specs=[vmem] * 6 + [smem, smem] + [vmem] * 5,
        out_specs=vmem,
        scratch_shapes=[VM((2, 3, 8, 2, BW, L), BF), VM((2, 3, 6, 2, BW, L), BF), VM((8 * BW, L), F32)],
        compiler_params=PARAMS,
    )(clip, up, down, up_early, down_early, gain2, widths, links, packed1, packed2, part1, part2, inner)


def solution(mesh):
    in_specs = (P("tm", "tile", None), P(), P(), P(), P(), P("tile"), P("tile", None))
    out_specs = P("tm", "tile", None)
    return jax.shard_map(local, mesh=mesh, in_specs=in_specs, out_specs=out_specs, check_vma=False)
```

time: 102 us -> 37.9 us (0.37)
  other arithmetic: 31.8 us -> 0 us
  waiting for transfers between devices: 15.6 us -> 1.21 us
  local copies, waits for them, and re-layouts: 18.8 us -> 4.48 us
  Pallas kernels: 0 us -> 14.3 us
  matrix products: 11.3 us -> 0 us
  starting transfers between devices: 21.4 us -> 16.9 us
  between operations: 2.7 us -> 0.75 us
    concatenate x18 -> x0, other arithmetic: 14.9 us -> none  [the longest x14 14.2 us: convolve(): jnp.concatenate([window_slab[:, :, tap_w:tap_w + cols_out] for tap_w in r...]
    ppermute x6 -> x5, waiting for transfers between devices: 15.6 us -> 1.21 us  [the longest x1 1.08 us: local(): up = lax.ppermute(bottom, 'tile', ups)]
    pallas_call x0 -> x3, Pallas kernels: none -> 14.3 us  [the longest x1 9.17 us: local(): pl.pallas_call(pre_kernel, out_shape=(VM((2, 9 * 256, 256), BF), VM((2, 9...]
    neg x2 -> x0, other arithmetic: 12.6 us -> none  [settle(): return jax.nn.silu(values * lax.rsqrt(mean_sq + 1e-06) * gain_vec)]
    dot_general x18 -> x0, matrix products: 11.3 us -> none  [convolve(): jnp.dot(tap_cols.reshape(-1, 3 * channels), weight[tap_t, tap_h], preferr...]
    slice x9 -> x0, local copies, waits for them, and re-layouts: 9.89 us -> none  [the longest x6 8.62 us: convolve(): window_slab[:, :, tap_w:tap_w + cols_out]]
    ppermute x6 -> x5, starting transfers between devices: 21.4 us -> 16.9 us  [the longest x1 8.92 us: local(): down = lax.ppermute(top, 'tile', downs)]
    unnamed x14 -> x12, local copies, waits for them, and re-layouts: 0.33 us -> 4.48 us
  transfers between devices with their start and end apart: 6 -> 5, of which waited for: 4 -> 2; matrix products, arithmetic and copies ran while one was open for 5% -> 0% of each run, Pallas kernels for 0% -> 26%
where the time goes in v1:
time: 37.9 us; the launch traced here: 37.6 us
  starting transfers between devices  16.9 us (45%)
  Pallas kernels  14.3 us (38%)
  local copies, waits for them, and re-layouts  4.48 us (12%)
  waiting for transfers between devices  1.21 us (3%)
  between operations  0.75 us (2%)
    pallas_call x1, Pallas kernels, local(): pl.pallas_call(pre_kernel, out_shape=(VM((2, 9 * 256, 256), BF), VM((2, 9...  9.17 us
    ppermute x1, starting transfers between devices, local(): down = lax.ppermute(top, 'tile', downs)  8.92 us
    unnamed x12, local copies, waits for them, and re-layouts  4.48 us
    pallas_call x1, Pallas kernels, local(): pl.pallas_call(post_kernel, out_shape=jax.ShapeDtypeStruct((4, 8, BW * C)...  4.32 us
    ppermute x1, starting transfers between devices, local(): up = lax.ppermute(bottom, 'tile', ups)  3.48 us
    ppermute x1, starting transfers between devices, local(): earlier = lax.ppermute(clip, 'tm', [(0, 1)])  1.88 us
    ppermute x1, starting transfers between devices, local(): up_early = lax.ppermute(up, 'tm', [(0, 1)])  1.29 us
    ppermute x1, starting transfers between devices, local(): down_early = lax.ppermute(down, 'tm', [(0, 1)])  1.29 us
  transfers between devices with their start and end apart: 5, of which 2 were waited for; matrix products, arithmetic and copies ran while one was open for 0% of the time, Pallas kernels for 26%

profile of v1, /device:TPU:6, one launch (start us, length us, event | category | flops | bytes accessed | tf_op | source)
XLA Modules:
  0.0 37.6 jit_solution(8501562077563434800)
XLA Ops:
  0.0 0.0 copy-start.5
  0.0 1.9 %collective-permute-start.4 = (bf16[4,8,6144]{2,1,0:T(8,128)(2,1)}, bf16[4,8,6144]{2,1,0:T(8,128)(2,1)S(1)}, u32[]{:S(2)}, u32[]{:S(2)}) collective-permute-start(bf16[4,8,6144]{2,1,0:T(8,128)(2,1)} %clip.5), channel_id=1, source_target_pairs={{0,1},{2,3},{4,5},{6,7},{8,9},{10,11},{12,13},{14,15},{16,17},{18,... | collective-permute-start | bytes 1179656 | tf_op jit(solution)/shard_map/ppermute | solution.py:160
  2.5 0.0 copy-start
  2.5 1.0 %copy-done = bf16[4,8,6144]{2,1,0:T(8,128)(2,1)S(1)} copy-done((bf16[4,8,6144]{2,1,0:T(8,128)(2,1)S(1)}, bf16[4,8,6144]{2,1,0:T(8,128)(2,1)}, u32[]{:S(2)}) %copy-start) | copy-done | bytes 393240
  3.5 0.0 copy-start.3
  3.5 0.7 %copy-done.3 = f32[96]{0:T(128)S(1)} copy-done((f32[96]{0:T(128)S(1)}, f32[96]{0:T(128)}, u32[]{:S(2)}) %copy-start.3) | copy-done | bytes 408
  4.2 0.8 %shard_map.73 = (bf16[4,2,64,128]{3,2,1,0:T(8,128)(2,1)S(1)}, bf16[4,2,64,128]{3,2,1,0:T(8,128)(2,1)S(1)}) custom-call(bf16[4,8,6144]{2,1,0:T(8,128)(2,1)S(1)} %copy-done, f32[1,96]{1,0:T(1,128)S(1)} %bitcast.2, s32[1]{0:T(128)S(6)} %copy.8.widths), custom_call_target="tpu_custom_call" | custom-call | tf_op jit(solution)/shard_map/pallas_call | solution.py:151
  5.0 3.5 %collective-permute-start = (bf16[4,2,64,128]{3,2,1,0:T(8,128)(2,1)S(1)}, bf16[4,2,64,128]{3,2,1,0:T(8,128)(2,1)S(1)}, u32[]{:S(2)}, u32[]{:S(2)}) collective-permute-start(bf16[4,2,64,128]{3,2,1,0:T(8,128)(2,1)S(1)} %get-tuple-element.12), channel_id=1, source_target_pairs={{0,2},{2,4},{4,6},{6,8},{8,10},{10,12},{12,14},{14,16},{16,18},{18... | collective-permute-start | bytes 393224 | tf_op jit(solution)/shard_map/ppermute | solution.py:159
  8.5 8.9 %collective-permute-start.1 = (bf16[4,2,64,128]{3,2,1,0:T(8,128)(2,1)S(1)}, bf16[4,2,64,128]{3,2,1,0:T(8,128)(2,1)S(1)}, u32[]{:S(2)}, u32[]{:S(2)}) collective-permute-start(bf16[4,2,64,128]{3,2,1,0:T(8,128)(2,1)S(1)} %get-tuple-element.13), channel_id=1, source_target_pairs={{2,0},{4,2},{6,4},{8,6},{10,8},{12,10},{14,12},{16,14},{18,16},{20... | collective-permute-start | bytes 393224 | tf_op jit(solution)/shard_map/ppermute | solution.py:161
  17.4 1.1 %collective-permute-done.up = bf16[4,2,64,128]{3,2,1,0:T(8,128)(2,1)S(1)} collective-permute-done((bf16[4,2,64,128]{3,2,1,0:T(8,128)(2,1)S(1)}, bf16[4,2,64,128]{3,2,1,0:T(8,128)(2,1)S(1)}, u32[]{:S(2)}, u32[]{:S(2)}) %collective-permute-start) | collective-permute-done | bytes 131104 | tf_op jit(solution)/shard_map/ppermute | solution.py:159
  18.5 1.3 %collective-permute-start.2 = (bf16[4,2,64,128]{3,2,1,0:T(8,128)(2,1)S(1)}, bf16[4,2,64,128]{3,2,1,0:T(8,128)(2,1)S(1)}, u32[]{:S(2)}, u32[]{:S(2)}) collective-permute-start(bf16[4,2,64,128]{3,2,1,0:T(8,128)(2,1)S(1)} %collective-permute-done.up), channel_id=1, source_target_pairs={{0,1},{2,3},{4,5},{6,7},{8,9},{10,11},{12,13},{14,15},{16,17},{18,... | collective-permute-start | bytes 393224 | tf_op jit(solution)/shard_map/ppermute | solution.py:176
  19.8 0.1 collective-permute-done.1.down
  19.9 1.3 %collective-permute-start.3 = (bf16[4,2,64,128]{3,2,1,0:T(8,128)(2,1)S(1)}, bf16[4,2,64,128]{3,2,1,0:T(8,128)(2,1)S(1)}, u32[]{:S(2)}, u32[]{:S(2)}) collective-permute-start(bf16[4,2,64,128]{3,2,1,0:T(8,128)(2,1)S(1)} %collective-permute-done.1.down), channel_id=1, source_target_pairs={{0,1},{2,3},{4,5},{6,7},{8,9},{10,11},{12,13},{14,15},{16,17},{18,... | collective-permute-start | bytes 393224 | tf_op jit(solution)/shard_map/ppermute | solution.py:177
  21.2 0.0 collective-permute-done.4.earlier
  21.2 0.0 copy-start.1
  21.2 1.1 %copy-done.1 = bf16[3,3,288,96]{3,2,1,0:T(8,128)(2,1)S(1)} copy-done((bf16[3,3,288,96]{3,2,1,0:T(8,128)(2,1)S(1)}, bf16[3,3,288,96]{3,2,1,0:T(8,128)(2,1)}, u32[]{:S(2)}) %copy-start.1) | copy-done | bytes 497688
  22.3 0.0 copy-start.2
  22.3 1.1 %copy-done.2 = bf16[3,3,288,96]{3,2,1,0:T(8,128)(2,1)S(1)} copy-done((bf16[3,3,288,96]{3,2,1,0:T(8,128)(2,1)S(1)}, bf16[3,3,288,96]{3,2,1,0:T(8,128)(2,1)}, u32[]{:S(2)}) %copy-start.2) | copy-done | bytes 497688
  23.4 0.0 copy-start.4
  23.4 0.7 %copy-done.4 = f32[96]{0:T(128)S(1)} copy-done((f32[96]{0:T(128)S(1)}, f32[96]{0:T(128)}, u32[]{:S(2)}) %copy-start.4) | copy-done | bytes 408
  24.0 9.2 %shard_map.74 = (bf16[2,2304,256]{2,1,0:T(8,128)(2,1)S(1)}, bf16[2,2304,256]{2,1,0:T(8,128)(2,1)S(1)}, f32[2,384,256]{2,1,0:T(8,128)S(1)}, f32[2,256,256]{2,1,0:T(8,128)S(1)}, f32[2,256,256]{2,1,0:T(8,128)S(1)}) custom-call(bf16[4,8,6144]{2,1,0:T(8,128)(2,1)S(1)} %copy-done, bf16[4,8,6144]{2,1,0:T(8,128)(2,1)S(1)} %collective-permute-done.4.earlier, ...), custom_call_target="tpu_custom_call" | custom-call | tf_op jit(solution)/shard_map/pallas_call | solution.py:162
  33.2 0.0 collective-permute-done.2.up_early
  33.2 0.0 collective-permute-done.3.down_early
  33.2 0.0 copy-done.5
  33.3 4.3 %shard_map.75 = bf16[4,8,6144]{2,1,0:T(8,128)(2,1)} custom-call(bf16[4,8,6144]{2,1,0:T(8,128)(2,1)S(1)} %copy-done, bf16[4,2,64,128]{3,2,1,0:T(8,128)(2,1)S(1)} %collective-permute-done.up, bf16[4,2,64,128]{3,2,1,0:T(8,128)(2,1)S(1)} %collective-permute-done.1.down, bf16[4,2,64,128]{3,2,1,0:T(8,128)(2,1)S(1)} %collective-permute-done.2.up_early, ...), custom_call_target="tpu_custom_call" | custom-call | tf_op jit(solution)/shard_map/pallas_call | solution.py:178
Async XLA Ops:
  0.0 33.2 %copy-start.5 = (s32[1,2]{1,0:T(1,128)S(1)}, s32[1,2]{1,0:T(1,128)}, u32[]{:S(2)}) copy-start(s32[1,2]{1,0:T(1,128)} %links.1) | copy-start | bytes 28
  0.0 21.2 %collective-permute-start.4 = (bf16[4,8,6144]{2,1,0:T(8,128)(2,1)}, bf16[4,8,6144]{2,1,0:T(8,128)(2,1)S(1)}, u32[]{:S(2)}, u32[]{:S(2)}) collective-permute-start(bf16[4,8,6144]{2,1,0:T(8,128)(2,1)} %clip.5), channel_id=1, source_target_pairs={{0,1},{2,3},{4,5},{6,7},{8,9},{10,11},{12,13},{14,15},{16,17},{18,... | collective-permute-start | bytes 1179656 | tf_op jit(solution)/shard_map/ppermute | solution.py:160
  2.5 1.0 %copy-start = (bf16[4,8,6144]{2,1,0:T(8,128)(2,1)S(1)}, bf16[4,8,6144]{2,1,0:T(8,128)(2,1)}, u32[]{:S(2)}) copy-start(bf16[4,8,6144]{2,1,0:T(8,128)(2,1)} %clip.5) | copy-start | bytes 1179652
  3.5 0.7 %copy-start.3 = (f32[96]{0:T(128)S(1)}, f32[96]{0:T(128)}, u32[]{:S(2)}) copy-start(f32[96]{0:T(128)} %param.8) | copy-start | bytes 1156
  5.0 13.5 %collective-permute-start = (bf16[4,2,64,128]{3,2,1,0:T(8,128)(2,1)S(1)}, bf16[4,2,64,128]{3,2,1,0:T(8,128)(2,1)S(1)}, u32[]{:S(2)}, u32[]{:S(2)}) collective-permute-start(bf16[4,2,64,128]{3,2,1,0:T(8,128)(2,1)S(1)} %get-tuple-element.12), channel_id=1, source_target_pairs={{0,2},{2,4},{4,6},{6,8},{8,10},{10,12},{12,14},{14,16},{16,18},{18... | collective-permute-start | bytes 393224 | tf_op jit(solution)/shard_map/ppermute | solution.py:159
  8.5 11.4 %collective-permute-start.1 = (bf16[4,2,64,128]{3,2,1,0:T(8,128)(2,1)S(1)}, bf16[4,2,64,128]{3,2,1,0:T(8,128)(2,1)S(1)}, u32[]{:S(2)}, u32[]{:S(2)}) collective-permute-start(bf16[4,2,64,128]{3,2,1,0:T(8,128)(2,1)S(1)} %get-tuple-element.13), channel_id=1, source_target_pairs={{2,0},{4,2},{6,4},{8,6},{10,8},{12,10},{14,12},{16,14},{18,16},{20... | collective-permute-start | bytes 393224 | tf_op jit(solution)/shard_map/ppermute | solution.py:161
  18.5 14.7 %collective-permute-start.2 = (bf16[4,2,64,128]{3,2,1,0:T(8,128)(2,1)S(1)}, bf16[4,2,64,128]{3,2,1,0:T(8,128)(2,1)S(1)}, u32[]{:S(2)}, u32[]{:S(2)}) collective-permute-start(bf16[4,2,64,128]{3,2,1,0:T(8,128)(2,1)S(1)} %collective-permute-done.up), channel_id=1, source_target_pairs={{0,1},{2,3},{4,5},{6,7},{8,9},{10,11},{12,13},{14,15},{16,17},{18,... | collective-permute-start | bytes 393224 | tf_op jit(solution)/shard_map/ppermute | solution.py:176
  19.9 13.3 %collective-permute-start.3 = (bf16[4,2,64,128]{3,2,1,0:T(8,128)(2,1)S(1)}, bf16[4,2,64,128]{3,2,1,0:T(8,128)(2,1)S(1)}, u32[]{:S(2)}, u32[]{:S(2)}) collective-permute-start(bf16[4,2,64,128]{3,2,1,0:T(8,128)(2,1)S(1)} %collective-permute-done.1.down), channel_id=1, source_target_pairs={{0,1},{2,3},{4,5},{6,7},{8,9},{10,11},{12,13},{14,15},{16,17},{18,... | collective-permute-start | bytes 393224 | tf_op jit(solution)/shard_map/ppermute | solution.py:177
  21.2 1.1 %copy-start.1 = (bf16[3,3,288,96]{3,2,1,0:T(8,128)(2,1)S(1)}, bf16[3,3,288,96]{3,2,1,0:T(8,128)(2,1)}, u32[]{:S(2)}) copy-start(bf16[3,3,288,96]{3,2,1,0:T(8,128)(2,1)} %weight1.1) | copy-start | bytes 1492996
  22.3 1.1 %copy-start.2 = (bf16[3,3,288,96]{3,2,1,0:T(8,128)(2,1)S(1)}, bf16[3,3,288,96]{3,2,1,0:T(8,128)(2,1)}, u32[]{:S(2)}) copy-start(bf16[3,3,288,96]{3,2,1,0:T(8,128)(2,1)} %weight2.1) | copy-start | bytes 1492996
  23.4 0.7 %copy-start.4 = (f32[96]{0:T(128)S(1)}, f32[96]{0:T(128)}, u32[]{:S(2)}) copy-start(f32[96]{0:T(128)} %param.10) | copy-start | bytes 1156

commit v2 on v1

v2 whole, which is shorter than its diff:
```python
import jax
import jax.numpy as jnp
from jax import lax
from jax.experimental import pallas as pl
from jax.experimental.pallas import tpu as pltpu
from jax.sharding import PartitionSpec as P

C = 96
L = 128
BW = 64
FAR = 32
BF = jnp.bfloat16
F32 = jnp.float32
VM = pltpu.VMEM
vmem = pl.BlockSpec(memory_space=pltpu.VMEM)
smem = pl.BlockSpec(memory_space=pltpu.SMEM)
hbm = pl.BlockSpec(memory_space=pltpu.HBM)
DMA = pltpu.SemaphoreType.DMA
PARAMS = pltpu.CompilerParams(vmem_limit_bytes=32 * 1024 * 1024)


def settle(x, half_gain):
    ms = jnp.sum(x * x, axis=-1, keepdims=True) * (1.0 / C)
    v = x * lax.rsqrt(ms + 1e-6) * half_gain
    return v + v * jnp.tanh(v)


def half_gain_of(gain):
    g = gain[...] * 0.5
    return jnp.concatenate([g, jnp.zeros((1, L - C), F32)], axis=1)


def spread(frame, scratch):
    pad = jnp.zeros((8, L - C), F32)
    for w in range(BW):
        piece = jnp.concatenate([frame[:, w * C : (w + 1) * C], pad], axis=1)
        scratch[pl.ds(w, 8, stride=BW), :] = piece


def shifts(h):
    row = lax.broadcasted_iota(jnp.int32, (BW, 1), 0)
    left = jnp.where(row == 0, 0.0, pltpu.roll(h, 1, 0))
    right = jnp.where(row == BW - 1, 0.0, pltpu.roll(h, BW - 1, 0))
    return left.astype(BF), h.astype(BF), right.astype(BF)


def put(ref, t, r, h):
    for k, v in enumerate(shifts(h)):
        ref[k, t, r] = v


def pack_weights(weight, packed):
    zero = jnp.zeros((L, L), BF)
    for i in range(3):
        for k in range(3):
            blocks = []
            for j in range(3):
                w = weight[i, j, k * C : (k + 1) * C, :]
                w = jnp.concatenate([w, jnp.zeros((C, L - C), BF)], axis=1)
                blocks.append(jnp.concatenate([w, jnp.zeros((L - C, L), BF)], axis=0))
            for half in range(2):
                for a in range(2):
                    for b in range(2):
                        j = 2 * half + a - b
                        row = (i * 3 + k) * 256 + a * L
                        packed[half, row : row + L, b * L : (b + 1) * L] = blocks[j] if 0 <= j <= 2 else zero


def half_conv(field, frames, row, packed, half):
    pieces = []
    for i in range(3):
        for k in range(3):
            for a in range(2):
                pieces.append(field[k, i : i + frames, row + a].reshape(frames * BW, L))
    return jnp.dot(jnp.concatenate(pieces, axis=1), packed[half], preferred_element_type=F32)


def start(*copies):
    copies = [pltpu.make_async_copy(*copy) for copy in copies]
    for copy in copies:
        copy.start()
    return copies


def column_mask(widths):
    return (lax.broadcasted_iota(jnp.int32, (BW, L), 0) < widths[0]).astype(F32)


def masks_of(widths, links):
    mask = column_mask(widths)
    return mask, mask * links[0, 0].astype(F32), mask * links[0, 1].astype(F32)


def is_even():
    return lax.rem(lax.axis_index("tile"), 2) == 0


def is_first():
    return lax.rem(lax.axis_index("tile"), FAR) == 0


def is_last():
    return lax.rem(lax.axis_index("tile"), FAR) == FAR - 1


def send_kernel(
    clip_hbm, gain1_hbm, weight1_hbm, gain2_hbm, weight2_hbm,
    clip, hidden, near, other, other_again, weight1, gain2, weight2, gain1, scratch, sems,
):
    gain_copy = start((gain1_hbm, gain1, sems.at[4]))[0]
    frames = start(*((clip_hbm.at[t], clip.at[t], sems.at[t]) for t in range(4)))
    pairs = ((weight1_hbm, weight1), (gain2_hbm, gain2), (weight2_hbm, weight2))
    rest = start(*((src, dst, sems.at[5 + n]) for n, (src, dst) in enumerate(pairs)))
    gain_copy.wait()
    g = half_gain_of(gain1)
    even = is_even()
    for t in range(4):
        frames[t].wait()
        spread(clip[t].astype(F32), scratch.at[t])
        rows = [settle(scratch[t, r * BW : (r + 1) * BW, :], g) for r in range(8)]
        for r in range(8):
            hidden[t, r] = rows[r].astype(BF)
        for r in range(2):
            near[t, r] = jnp.where(even, rows[6 + r], rows[r]).astype(BF)
            away = jnp.where(even, rows[r], rows[6 + r]).astype(BF)
            other[t, r] = away
            other_again[t, r] = away
    for copy in rest:
        copy.wait()


def pre_body(
    hidden, earlier, weight1, gain2, weight2, widths,
    packed1, packed2, part1, part2, inner, x1, x2,
):
    has_earlier = (lax.axis_index("tm") > 0).astype(F32)
    mask = column_mask(widths)
    early_mask = mask * has_earlier
    g2 = half_gain_of(gain2)
    for t in range(8):
        for r in range(8):
            h = earlier[t, r].astype(F32) * early_mask if t < 4 else hidden[t - 4, r].astype(F32) * mask
            put(x1, t, r, h)
    pack_weights(weight1, packed1)
    pack_weights(weight2, packed2)
    part1[0] = half_conv(x1, 6, 0, packed1, 1)
    part1[1] = half_conv(x1, 6, 6, packed1, 0)
    for p in range(1, 4):
        acc = half_conv(x1, 6, 2 * p - 2, packed1, 0) + half_conv(x1, 6, 2 * p, packed1, 1)
        for t in range(6):
            m = early_mask if t < 2 else mask
            for b in range(2):
                put(x2, t, 2 * p - 2 + b, settle(acc[t * BW : (t + 1) * BW, b * L : (b + 1) * L], g2) * m)
    part2[0] = half_conv(x2, 4, 0, packed2, 1)
    part2[1] = half_conv(x2, 4, 4, packed2, 0)
    for q in range(1, 3):
        inner[q - 1] = half_conv(x2, 4, 2 * q - 2, packed2, 0) + half_conv(x2, 4, 2 * q, packed2, 1)


def pre_first_kernel(*refs):
    @pl.when(is_first())
    def _():
        pre_body(*refs[:6], *refs[8:])


def pre_rest_kernel(*refs):
    @pl.when(jnp.logical_not(is_first()))
    def _():
        pre_body(*refs[:6], *refs[11:])


def halo_kernel(near, other, other_far, halos):
    even = is_even().astype(jnp.int32)
    halos[even] = near[...]

    @pl.when(is_first())
    def _():
        halos[1 - even] = other_far[...]

    @pl.when(jnp.logical_not(is_first()))
    def _():
        halos[1 - even] = other[...]


def post_kernel(
    clip, halos, early_halos, below, early_below, gain2, widths, links, packed1, packed2, part1, part2, inner,
    out_hbm, x1, x2, scratch, out, sems,
):
    g2 = half_gain_of(gain2)
    last = is_last()
    has_earlier = (lax.axis_index("tm") > 0).astype(F32)
    masks = masks_of(widths, links)
    early_masks = [m * has_earlier for m in masks]
    live = lax.broadcasted_iota(jnp.int32, (8, BW * C), 1) < widths[0] * C
    for side in range(2):
        for t in range(8):
            for r in range(2):
                rows, far = (early_halos, early_below) if t < 4 else (halos, below)
                h = rows[side, t % 4, r].astype(F32)
                if side == 1:
                    h = jnp.where(last, far[t % 4, r].astype(F32), h)
                put(x1.at[side], t, r, h * (early_masks if t < 4 else masks)[1 + side])
        acc = part1[side] + half_conv(x1.at[side], 6, 0, packed1, side)
        for t in range(6):
            for b in range(2):
                m = (early_masks if t < 2 else masks)[1 + side if b == side else 0]
                put(x2.at[side], t, b, settle(acc[t * BW : (t + 1) * BW, b * L : (b + 1) * L], g2) * m)
    outer_rows = [part2[s] + half_conv(x2.at[s], 4, 0, packed2, s) for s in range(2)]
    copies = []
    for t in range(4):
        for q in range(4):
            acc = inner[q - 1] if q in (1, 2) else outer_rows[q // 3]
            for b in range(2):
                r = 2 * q + b
                scratch[t, r * BW : (r + 1) * BW, :] = acc[t * BW : (t + 1) * BW, b * L : (b + 1) * L]
        pieces = [scratch[t, pl.ds(w, 8, stride=BW), :][:, :C] for w in range(BW)]
        y = clip[t].astype(F32) + jnp.concatenate(pieces, axis=1)
        out[t] = jnp.where(live, y, 0.0).astype(BF)
        copies += start((out.at[t], out_hbm.at[t], sems.at[t]))
    for copy in copies:
        copy.wait()


def local(clip, gain1, weight1, gain2, weight2, widths, links):
    tiles = lax.axis_size("tile")
    near_pairs = [(i, i ^ 1) for i in range(tiles)]
    last = [i for i in range(FAR - 1, tiles - 1, FAR)]
    ends = {n * FAR + m: (n ^ 1) * FAR + m for n in range(tiles // FAR) for m in (0, FAR - 1)}
    other_pairs = [(i, ends.get(i, ((i + 1) ^ 1) - 1)) for i in range(tiles)]
    cores = [(0, 1), (1, 0)]
    gain1, gain2 = gain1.reshape(1, C), gain2.reshape(1, C)
    clip, gain1, weight1, gain2, weight2 = (
        pltpu.with_memory_space_constraint(x, pltpu.HBM) for x in (clip, gain1, weight1, gain2, weight2)
    )
    edge = VM((4, 2, BW, L), BF)
    weight = VM((3, 3, 3 * C, C), BF)
    clip, hidden, near, other, other_again, weight1, gain2, weight2 = pl.pallas_call(
        send_kernel,
        out_shape=(
            VM((4, 8, BW * C), BF), VM((4, 8, BW, L), BF), edge, edge, edge, weight, VM((1, C), F32), weight,
        ),
        in_specs=[hbm] * 5,
        out_specs=(vmem,) * 8,
        scratch_shapes=[VM((1, C), F32), VM((4, 8 * BW, L), F32), DMA((8,))],
        compiler_params=PARAMS,
    )(clip, gain1, weight1, gain2, weight2)
    from_far = lax.ppermute(other, "tile", [(i, i + 1) for i in last])
    from_near = lax.ppermute(near, "tile", near_pairs)
    from_other = lax.ppermute(other, "tile", other_pairs)
    earlier = lax.ppermute(hidden, "tm", cores)
    state = (
        VM((2, 9 * 256, 256), BF),
        VM((2, 9 * 256, 256), BF),
        VM((2, 6 * BW, 256), F32),
        VM((2, 4 * BW, 256), F32),
        VM((2, 4 * BW, 256), F32),
    )
    inputs = (hidden, earlier, weight1, gain2, weight2, widths)
    specs = [vmem] * 5 + [smem]
    scratch = [
        VM((3, 8, 8, BW, L), BF),
        VM((3, 6, 6, BW, L), BF),
    ]
    first = pl.pallas_call(
        pre_first_kernel,
        out_shape=(edge, *state),
        in_specs=specs + [vmem],
        out_specs=(vmem,) * 6,
        scratch_shapes=scratch,
        input_output_aliases={6: 0},
        compiler_params=PARAMS,
    )(*inputs, other_again)
    below = lax.ppermute(first[0], "tile", [(i + 1, i) for i in last])
    made = pl.pallas_call(
        pre_rest_kernel,
        out_shape=state,
        in_specs=specs + [vmem] * 5,
        out_specs=(vmem,) * 5,
        scratch_shapes=scratch,
        input_output_aliases={6 + n: n for n in range(5)},
        compiler_params=PARAMS,
    )(*inputs, *first[1:])
    from_far, from_near, from_other, made = lax.optimization_barrier((from_far, from_near, from_other, made))
    halos = pl.pallas_call(
        halo_kernel,
        out_shape=VM((2, 4, 2, BW, L), BF),
        in_specs=[vmem] * 3,
        out_specs=vmem,
        compiler_params=PARAMS,
    )(from_near, from_other, from_far)
    below, halos = lax.optimization_barrier((below, halos))
    early_halos = lax.ppermute(halos, "tm", cores)
    early_below = lax.ppermute(below, "tm", cores)
    return pl.pallas_call(
        post_kernel,
        out_shape=pltpu.HBM((4, 8, BW * C), BF),
        in_specs=[vmem] * 6 + [smem, smem] + [vmem] * 5,
        out_specs=hbm,
        scratch_shapes=[
            VM((2, 3, 8, 2, BW, L), BF),
            VM((2, 3, 6, 2, BW, L), BF),
            VM((4, 8 * BW, L), F32),
            VM((4, 8, BW * C), BF),
            DMA((4,)),
        ],
        compiler_params=PARAMS,
    )(clip, halos, early_halos, below, early_below, gain2, widths, links, *made)


def solution(mesh):
    in_specs = (P("tm", "tile", None), P(), P(), P(), P(), P("tile"), P("tile", None))
    out_specs = P("tm", "tile", None)
    return jax.shard_map(local, mesh=mesh, in_specs=in_specs, out_specs=out_specs, check_vma=False)
```

time: 37.9 us -> 25.9 us (0.68)
  the two profiles are of different devices: /device:TPU:6 before, /device:TPU:3 now
where the time goes in v2:
time: 25.9 us; the launch traced here: 25.8 us
  Pallas kernels  14.1 us (54%)
  starting transfers between devices  7.17 us (28%)
  waiting for transfers between devices  3.62 us (14%)
  between operations  0.91 us (4%)
    pallas_call x1, Pallas kernels, local(): pl.pallas_call(pre_first_kernel, out_shape=(edge, *state), in_specs=specs...  7.24 us
    pallas_call x1, Pallas kernels, local(): pl.pallas_call(post_kernel, out_shape=pltpu.HBM((4, 8, BW * C), BF), in_s...  4.17 us
    pallas_call x1, Pallas kernels, local(): pl.pallas_call(send_kernel, out_shape=(VM((4, 8, BW * C), BF), VM((4, 8,...  2.42 us
    ppermute x1, waiting for transfers between devices, local(): below = lax.ppermute(first[0], 'tile', [(i + 1, i) for i in last])  2.26 us
    ppermute x1, starting transfers between devices, local(): below = lax.ppermute(first[0], 'tile', [(i + 1, i) for i in last])  1.94 us
    ppermute x1, starting transfers between devices, local(): from_other = lax.ppermute(other, 'tile', other_pairs)  1.45 us
    ppermute x1, waiting for transfers between devices, local(): early_below = lax.ppermute(below, 'tm', cores)  1.35 us
    ppermute x1, starting transfers between devices, local(): from_far = lax.ppermute(other, 'tile', [(i, i + 1) for i in last])  1.28 us
  transfers between devices with their start and end apart: 7, of which 2 were waited for; matrix products, arithmetic and copies ran while one was open for 0% of the time, Pallas kernels for 29%

profile of v2, /device:TPU:3, one launch (start us, length us, event | category | flops | bytes accessed | tf_op | source)
XLA Modules:
  0.0 25.8 jit_solution(17743475285794327678)
XLA Ops:
  0.0 2.4 %shard_map.73 = (bf16[4,8,6144]{2,1,0:T(8,128)(2,1)S(1)}, bf16[4,8,64,128]{3,2,1,0:T(8,128)(2,1)S(1)}, bf16[4,2,64,128]{3,2,1,0:T(8,128)(2,1)S(1)}, bf16[4,2,64,...) custom-call(bf16[4,8,6144]{2,1,0:T(8,128)(2,1)} %clip_hbm.1, ...), custom_call_target="tpu_custom_call" | custom-call | tf_op jit(solution)/shard_map/pallas_call | solution.py:237
  2.4 0.8 %collective-permute-start = (bf16[4,8,64,128]{3,2,1,0:T(8,128)(2,1)S(1)}, bf16[4,8,64,128]{3,2,1,0:T(8,128)(2,1)S(1)}, u32[]{:S(2)}, u32[]{:S(2)}) collective-permute-start(bf16[4,8,64,128]{3,2,1,0:T(8,128)(2,1)S(1)} %get-tuple-element.35.refs_0_), channel_id=1, source_target_pairs={{0,1},{1,0},{2,3},{3,2},{4,5},{5,4},{6,7},{7,6},{8,9},{9,8},{10,11... | collective-permute-start | bytes 1572872 | tf_op jit(solution)/shard_map/ppermute | solution.py:250
  3.2 1.3 %collective-permute-start.2 = (bf16[4,2,64,128]{3,2,1,0:T(8,128)(2,1)S(1)}, bf16[4,2,64,128]{3,2,1,0:T(8,128)(2,1)S(1)}, u32[]{:S(2)}, u32[]{:S(2)}) collective-permute-start(bf16[4,2,64,128]{3,2,1,0:T(8,128)(2,1)S(1)} %get-tuple-element.41), channel_id=1, source_target_pairs={{62,64},{126,128},{190,192},{63,65},{127,129},{191,193}} | collective-permute-start | bytes 393224 | tf_op jit(solution)/shard_map/ppermute | solution.py:247
  4.5 1.5 %collective-permute-start.4 = (bf16[4,2,64,128]{3,2,1,0:T(8,128)(2,1)S(1)}, bf16[4,2,64,128]{3,2,1,0:T(8,128)(2,1)S(1)}, u32[]{:S(2)}, u32[]{:S(2)}) collective-permute-start(bf16[4,2,64,128]{3,2,1,0:T(8,128)(2,1)S(1)} %get-tuple-element.41), channel_id=1, source_target_pairs={{0,64},{2,4},{4,2},{6,8},{8,6},{10,12},{12,10},{14,16},{16,14},{18... | collective-permute-start | bytes 393224 | tf_op jit(solution)/shard_map/ppermute | solution.py:249
  5.9 0.6 %collective-permute-start.3 = (bf16[4,2,64,128]{3,2,1,0:T(8,128)(2,1)S(1)}, bf16[4,2,64,128]{3,2,1,0:T(8,128)(2,1)S(1)}, u32[]{:S(2)}, u32[]{:S(2)}) collective-permute-start(bf16[4,2,64,128]{3,2,1,0:T(8,128)(2,1)S(1)} %get-tuple-element.42), channel_id=1, source_target_pairs={{0,2},{2,0},{4,6},{6,4},{8,10},{10,8},{12,14},{14,12},{16,18},{18,... | collective-permute-start | bytes 393224 | tf_op jit(solution)/shard_map/ppermute | solution.py:248
  7.2 0.0 collective-permute-done.refs_1_
  7.2 7.2 %shard_map.74 = (bf16[4,2,64,128]{3,2,1,0:T(8,128)(2,1)S(1)}, bf16[2,2304,256]{2,1,0:T(8,128)(2,1)S(1)}, bf16[2,2304,256]{2,1,0:T(8,128)(2,1)S(1)}, f32[2,384,25...) custom-call(bf16[4,8,64,128]{3,2,1,0:T(8,128)(2,1)S(1)} %get-tuple-e, ...), custom_call_target="tpu_custom_call", output_to_operand_aliasing={{0}: (6, {})} | custom-call | tf_op jit(solution)/shard_map/pallas_call | solution.py:264
  14.4 1.9 %collective-permute-start.1 = (bf16[4,2,64,128]{3,2,1,0:T(8,128)(2,1)S(1)}, bf16[4,2,64,128]{3,2,1,0:T(8,128)(2,1)S(1)}, u32[]{:S(2)}, u32[]{:S(2)}) collective-permute-start(bf16[4,2,64,128]{3,2,1,0:T(8,128)(2,1)S(1)} %get-tuple-element.40), channel_id=1, source_target_pairs={{64,62},{128,126},{192,190},{65,63},{129,127},{193,191}} | collective-permute-start | bytes 393224 | tf_op jit(solution)/shard_map/ppermute | solution.py:273
  16.4 0.0 copy-start
  16.4 0.2 shard_map.75
  16.6 0.0 collective-permute-done.2.other_far
  16.6 0.0 collective-permute-done.4.other
  16.6 0.0 collective-permute-done.3.near
  16.7 2.3 %collective-permute-done.1.below = bf16[4,2,64,128]{3,2,1,0:T(8,128)(2,1)S(1)} collective-permute-done((bf16[4,2,64,128]{3,2,1,0:T(8,128)(2,1)S(1)}, bf16[4,2,64,128]{3,2,1,0:T(8,128)(2,1)S(1)}, u32[]{:S(2)}, u32[]{:S(2)}) %collective-permute-start.1) | collective-permute-done | bytes 131104 | tf_op jit(solution)/shard_map/ppermute | solution.py:273
  18.9 1.1 %collective-permute-start.5 = (bf16[2,4,2,64,128]{4,3,2,1,0:T(8,128)(2,1)S(1)}, bf16[2,4,2,64,128]{4,3,2,1,0:T(8,128)(2,1)S(1)}, u32[]{:S(2)}, u32[]{:S(2)}) collective-permute-start(bf16[2,4,2,64,128]{4,3,2,1,0:T(8,128)(2,1)S(1)} %shard_map.76.halos), channel_id=1, source_target_pairs={{0,1},{1,0},{2,3},{3,2},{4,5},{5,4},{6,7},{7,6},{8,9},{9,8},{10,11... | collective-permute-start | bytes 786440 | tf_op jit(solution)/shard_map/ppermute | solution.py:292
  20.1 0.0 collective-permute-start.6
  20.1 1.3 %collective-permute-done.6.early_below = bf16[4,2,64,128]{3,2,1,0:T(8,128)(2,1)S(1)} collective-permute-done((bf16[4,2,64,128]{3,2,1,0:T(8,128)(2,1)S(1)}, bf16[4,2,64,128]{3,2,1,0:T(8,128)(2,1)S(1)}, u32[]{:S(2)}, u32[]{:S(2)}) %collective-permute-start.6) | collective-permute-done | bytes 131104 | tf_op jit(solution)/shard_map/ppermute | solution.py:293
  21.4 0.0 collective-permute-done.5.early_halos
  21.4 0.0 copy-done
  21.4 4.2 %shard_map.77 = bf16[4,8,6144]{2,1,0:T(8,128)(2,1)} custom-call(bf16[4,8,6144]{2,1,0:T(8,128)(2,1)S(1)} %get-tuple-element.34.clip, bf16[2,4,2,64,128]{4,3,2,1,0:T(8,128)(2,1)S(1)} %shard_map.76.halos, bf16[2,4,2,64,128]{4,3,2,1,0:T(8,128)(2,1)S(1)} %collective-permute-done.5.early_halos, bf16[4,2,64,128]{3,2,1,0:T(8,128)(2,1)S(1)} %collective-permute-done.1.below, ...), custom_call_target="tpu_custom_call" | custom-call | tf_op jit(solution)/shard_map/pallas_call | solution.py:294
  (1 shorter events, 0.0 us)
Async XLA Ops:
  2.4 4.8 %collective-permute-start = (bf16[4,8,64,128]{3,2,1,0:T(8,128)(2,1)S(1)}, bf16[4,8,64,128]{3,2,1,0:T(8,128)(2,1)S(1)}, u32[]{:S(2)}, u32[]{:S(2)}) collective-permute-start(bf16[4,8,64,128]{3,2,1,0:T(8,128)(2,1)S(1)} %get-tuple-element.35.refs_0_), channel_id=1, source_target_pairs={{0,1},{1,0},{2,3},{3,2},{4,5},{5,4},{6,7},{7,6},{8,9},{9,8},{10,11... | collective-permute-start | bytes 1572872 | tf_op jit(solution)/shard_map/ppermute | solution.py:250
  3.2 13.4 %collective-permute-start.2 = (bf16[4,2,64,128]{3,2,1,0:T(8,128)(2,1)S(1)}, bf16[4,2,64,128]{3,2,1,0:T(8,128)(2,1)S(1)}, u32[]{:S(2)}, u32[]{:S(2)}) collective-permute-start(bf16[4,2,64,128]{3,2,1,0:T(8,128)(2,1)S(1)} %get-tuple-element.41), channel_id=1, source_target_pairs={{62,64},{126,128},{190,192},{63,65},{127,129},{191,193}} | collective-permute-start | bytes 393224 | tf_op jit(solution)/shard_map/ppermute | solution.py:247
  4.5 12.2 %collective-permute-start.4 = (bf16[4,2,64,128]{3,2,1,0:T(8,128)(2,1)S(1)}, bf16[4,2,64,128]{3,2,1,0:T(8,128)(2,1)S(1)}, u32[]{:S(2)}, u32[]{:S(2)}) collective-permute-start(bf16[4,2,64,128]{3,2,1,0:T(8,128)(2,1)S(1)} %get-tuple-element.41), channel_id=1, source_target_pairs={{0,64},{2,4},{4,2},{6,8},{8,6},{10,12},{12,10},{14,16},{16,14},{18... | collective-permute-start | bytes 393224 | tf_op jit(solution)/shard_map/ppermute | solution.py:249
  5.9 10.7 %collective-permute-start.3 = (bf16[4,2,64,128]{3,2,1,0:T(8,128)(2,1)S(1)}, bf16[4,2,64,128]{3,2,1,0:T(8,128)(2,1)S(1)}, u32[]{:S(2)}, u32[]{:S(2)}) collective-permute-start(bf16[4,2,64,128]{3,2,1,0:T(8,128)(2,1)S(1)} %get-tuple-element.42), channel_id=1, source_target_pairs={{0,2},{2,0},{4,6},{6,4},{8,10},{10,8},{12,14},{14,12},{16,18},{18,... | collective-permute-start | bytes 393224 | tf_op jit(solution)/shard_map/ppermute | solution.py:248
  14.4 4.5 %collective-permute-start.1 = (bf16[4,2,64,128]{3,2,1,0:T(8,128)(2,1)S(1)}, bf16[4,2,64,128]{3,2,1,0:T(8,128)(2,1)S(1)}, u32[]{:S(2)}, u32[]{:S(2)}) collective-permute-start(bf16[4,2,64,128]{3,2,1,0:T(8,128)(2,1)S(1)} %get-tuple-element.40), channel_id=1, source_target_pairs={{64,62},{128,126},{192,190},{65,63},{129,127},{193,191}} | collective-permute-start | bytes 393224 | tf_op jit(solution)/shard_map/ppermute | solution.py:273
  16.4 5.0 %copy-start = (s32[1,2]{1,0:T(1,128)S(1)}, s32[1,2]{1,0:T(1,128)}, u32[]{:S(2)}) copy-start(s32[1,2]{1,0:T(1,128)} %links.1) | copy-start | bytes 28
  18.9 2.5 %collective-permute-start.5 = (bf16[2,4,2,64,128]{4,3,2,1,0:T(8,128)(2,1)S(1)}, bf16[2,4,2,64,128]{4,3,2,1,0:T(8,128)(2,1)S(1)}, u32[]{:S(2)}, u32[]{:S(2)}) collective-permute-start(bf16[2,4,2,64,128]{4,3,2,1,0:T(8,128)(2,1)S(1)} %shard_map.76.halos), channel_id=1, source_target_pairs={{0,1},{1,0},{2,3},{3,2},{4,5},{5,4},{6,7},{7,6},{8,9},{9,8},{10,11... | collective-permute-start | bytes 786440 | tf_op jit(solution)/shard_map/ppermute | solution.py:292
  20.1 1.3 %collective-permute-start.6 = (bf16[4,2,64,128]{3,2,1,0:T(8,128)(2,1)S(1)}, bf16[4,2,64,128]{3,2,1,0:T(8,128)(2,1)S(1)}, u32[]{:S(2)}, u32[]{:S(2)}) collective-permute-start(bf16[4,2,64,128]{3,2,1,0:T(8,128)(2,1)S(1)} %collective-permute-done.1.below), channel_id=1, source_target_pairs={{0,1},{1,0},{2,3},{3,2},{4,5},{5,4},{6,7},{7,6},{8,9},{9,8},{10,11... | collective-permute-start | bytes 393224 | tf_op jit(solution)/shard_map/ppermute | solution.py:293

commit v3 on v2

--- a/solution.py
+++ b/solution.py
@@ -9,6 +9,7 @@
 L = 128
 BW = 64
 FAR = 32
+STEP = BW + 8
 BF = jnp.bfloat16
 F32 = jnp.float32
 VM = pltpu.VMEM
@@ -34,7 +35,7 @@
     pad = jnp.zeros((8, L - C), F32)
     for w in range(BW):
         piece = jnp.concatenate([frame[:, w * C : (w + 1) * C], pad], axis=1)
-        scratch[pl.ds(w, 8, stride=BW), :] = piece
+        scratch[pl.ds(w, 8, stride=STEP), :] = piece
 
 
 def shifts(h):
@@ -117,7 +118,7 @@
     for t in range(4):
         frames[t].wait()
         spread(clip[t].astype(F32), scratch.at[t])
-        rows = [settle(scratch[t, r * BW : (r + 1) * BW, :], g) for r in range(8)]
+        rows = [settle(scratch[t, r * STEP : r * STEP + BW, :], g) for r in range(8)]
         for r in range(8):
             hidden[t, r] = rows[r].astype(BF)
         for r in range(2):
@@ -137,24 +138,41 @@
     mask = column_mask(widths)
     early_mask = mask * has_earlier
     g2 = half_gain_of(gain2)
-    for t in range(8):
-        for r in range(8):
-            h = earlier[t, r].astype(F32) * early_mask if t < 4 else hidden[t - 4, r].astype(F32) * mask
-            put(x1, t, r, h)
-    pack_weights(weight1, packed1)
-    pack_weights(weight2, packed2)
-    part1[0] = half_conv(x1, 6, 0, packed1, 1)
-    part1[1] = half_conv(x1, 6, 6, packed1, 0)
-    for p in range(1, 4):
-        acc = half_conv(x1, 6, 2 * p - 2, packed1, 0) + half_conv(x1, 6, 2 * p, packed1, 1)
+
+    def fill(rows):
+        for t in range(8):
+            for r in rows:
+                h = earlier[t, r].astype(F32) * early_mask if t < 4 else hidden[t - 4, r].astype(F32) * mask
+                put(x1, t, r, h)
+
+    def first_pair(p):
+        return half_conv(x1, 6, 2 * p - 2, packed1, 0) + half_conv(x1, 6, 2 * p, packed1, 1)
+
+    def settle_pair(p, acc):
         for t in range(6):
             m = early_mask if t < 2 else mask
             for b in range(2):
                 put(x2, t, 2 * p - 2 + b, settle(acc[t * BW : (t + 1) * BW, b * L : (b + 1) * L], g2) * m)
+
+    def second_pair(q):
+        inner[q - 1] = half_conv(x2, 4, 2 * q - 2, packed2, 0) + half_conv(x2, 4, 2 * q, packed2, 1)
+
+    fill(range(4))
+    pack_weights(weight1, packed1)
+    acc1 = first_pair(1)
+    fill(range(4, 8))
+    acc2 = first_pair(2)
+    settle_pair(1, acc1)
+    acc3 = first_pair(3)
+    settle_pair(2, acc2)
+    pack_weights(weight2, packed2)
+    part1[0] = half_conv(x1, 6, 0, packed1, 1)
+    settle_pair(3, acc3)
+    second_pair(1)
+    part1[1] = half_conv(x1, 6, 6, packed1, 0)
     part2[0] = half_conv(x2, 4, 0, packed2, 1)
+    second_pair(2)
     part2[1] = half_conv(x2, 4, 4, packed2, 0)
-    for q in range(1, 3):
-        inner[q - 1] = half_conv(x2, 4, 2 * q - 2, packed2, 0) + half_conv(x2, 4, 2 * q, packed2, 1)
 
 
 def pre_first_kernel(*refs):
@@ -169,21 +187,27 @@
         pre_body(*refs[:6], *refs[11:])
 
 
-def halo_kernel(near, other, other_far, halos):
-    even = is_even().astype(jnp.int32)
-    halos[even] = near[...]
-
-    @pl.when(is_first())
+def halo_kernel(near, other, other_far, above, below):
+    @pl.when(is_even())
     def _():
-        halos[1 - even] = other_far[...]
-
-    @pl.when(jnp.logical_not(is_first()))
+        below[...] = near[...]
+
+        @pl.when(is_first())
+        def _():
+            above[...] = other_far[...]
+
+        @pl.when(jnp.logical_not(is_first()))
+        def _():
+            above[...] = other[...]
+
+    @pl.when(jnp.logical_not(is_even()))
     def _():
-        halos[1 - even] = other[...]
+        above[...] = near[...]
+        below[...] = other[...]
 
 
 def post_kernel(
-    clip, halos, early_halos, below, early_below, gain2, widths, links, packed1, packed2, part1, part2, inner,
+    clip, above, below, early_above, early_below, far_below, far_early_below, gain2, widths, links, packed1, packed2, part1, part2, inner,
     out_hbm, x1, x2, scratch, out, sems,
 ):
     g2 = half_gain_of(gain2)
@@ -195,9 +219,10 @@
     for side in range(2):
         for t in range(8):
             for r in range(2):
-                rows, far = (early_halos, early_below) if t < 4 else (halos, below)
-                h = rows[side, t % 4, r].astype(F32)
+                rows = ((early_above, early_below) if t < 4 else (above, below))[side]
+                h = rows[t % 4, r].astype(F32)
                 if side == 1:
+                    far = far_early_below if t < 4 else far_below
                     h = jnp.where(last, far[t % 4, r].astype(F32), h)
                 put(x1.at[side], t, r, h * (early_masks if t < 4 else masks)[1 + side])
         acc = part1[side] + half_conv(x1.at[side], 6, 0, packed1, side)
@@ -212,8 +237,8 @@
             acc = inner[q - 1] if q in (1, 2) else outer_rows[q // 3]
             for b in range(2):
                 r = 2 * q + b
-                scratch[t, r * BW : (r + 1) * BW, :] = acc[t * BW : (t + 1) * BW, b * L : (b + 1) * L]
-        pieces = [scratch[t, pl.ds(w, 8, stride=BW), :][:, :C] for w in range(BW)]
+                scratch[t, r * STEP : r * STEP + BW, :] = acc[t * BW : (t + 1) * BW, b * L : (b + 1) * L]
+        pieces = [scratch[t, pl.ds(w, 8, stride=STEP), :][:, :C] for w in range(BW)]
         y = clip[t].astype(F32) + jnp.concatenate(pieces, axis=1)
         out[t] = jnp.where(live, y, 0.0).astype(BF)
         copies += start((out.at[t], out_hbm.at[t], sems.at[t]))
@@ -241,7 +266,7 @@
         ),
         in_specs=[hbm] * 5,
         out_specs=(vmem,) * 8,
-        scratch_shapes=[VM((1, C), F32), VM((4, 8 * BW, L), F32), DMA((8,))],
+        scratch_shapes=[VM((1, C), F32), VM((4, 8 * STEP, L), F32), DMA((8,))],
         compiler_params=PARAMS,
     )(clip, gain1, weight1, gain2, weight2)
     from_far = lax.ppermute(other, "tile", [(i, i + 1) for i in last])
@@ -270,7 +295,7 @@
         input_output_aliases={6: 0},
         compiler_params=PARAMS,
     )(*inputs, other_again)
-    below = lax.ppermute(first[0], "tile", [(i + 1, i) for i in last])
+    far_below = lax.ppermute(first[0], "tile", [(i + 1, i) for i in last])
     made = pl.pallas_call(
         pre_rest_kernel,
         out_shape=state,
@@ -281,30 +306,32 @@
         compiler_params=PARAMS,
     )(*inputs, *first[1:])
     from_far, from_near, from_other, made = lax.optimization_barrier((from_far, from_near, from_other, made))
-    halos = pl.pallas_call(
+    above, below = pl.pallas_call(
         halo_kernel,
-        out_shape=VM((2, 4, 2, BW, L), BF),
+        out_shape=(edge, edge),
         in_specs=[vmem] * 3,
-        out_specs=vmem,
+        out_specs=(vmem, vmem),
         compiler_params=PARAMS,
     )(from_near, from_other, from_far)
-    below, halos = lax.optimization_barrier((below, halos))
-    early_halos = lax.ppermute(halos, "tm", cores)
+    early_above = lax.ppermute(above, "tm", cores)
     early_below = lax.ppermute(below, "tm", cores)
+    far_early_below = lax.ppermute(far_below, ("tile", "tm"), [(2 * i, 2 * i + 1) for i in last])
     return pl.pallas_call(
         post_kernel,
         out_shape=pltpu.HBM((4, 8, BW * C), BF),
-        in_specs=[vmem] * 6 + [smem, smem] + [vmem] * 5,
+        in_specs=[vmem] * 8 + [smem, smem] + [vmem] * 5,
         out_specs=hbm,
         scratch_shapes=[
             VM((2, 3, 8, 2, BW, L), BF),
             VM((2, 3, 6, 2, BW, L), BF),
-            VM((4, 8 * BW, L), F32),
+            VM((4, 8 * STEP, L), F32),
             VM((4, 8, BW * C), BF),
             DMA((4,)),
         ],
         compiler_params=PARAMS,
-    )(clip, halos, early_halos, below, early_below, gain2, widths, links, *made)
+    )(
+        clip, above, below, early_above, early_below, far_below, far_early_below, gain2, widths, links, *made
+    )
 
 
 def solution(mesh):

time: 25.9 us -> 24.4 us (0.942)
  the two profiles are of different devices: /device:TPU:3 before, /device:TPU:249 now
where the time goes in v3:
time: 24.4 us; the launch traced here: 24.3 us
  Pallas kernels  12.7 us (52%)
  starting transfers between devices  6.52 us (27%)
  waiting for transfers between devices  4.16 us (17%)
  between operations  0.93 us (4%)
    pallas_call x1, Pallas kernels, local(): pl.pallas_call(pre_rest_kernel, out_shape=state, in_specs=specs + [vmem]...  6.69 us
    pallas_call x1, Pallas kernels, local(): pl.pallas_call(post_kernel, out_shape=pltpu.HBM((4, 8, BW * C), BF), in_s...  3.76 us
    ppermute x1, waiting for transfers between devices, local(): far_below = lax.ppermute(first[0], 'tile', [(i + 1, i) for i in last])  2.21 us
    pallas_call x1, Pallas kernels, local(): pl.pallas_call(send_kernel, out_shape=(VM((4, 8, BW * C), BF), VM((4, 8,...  2.15 us
    ppermute x1, waiting for transfers between devices, local(): lax.ppermute(far_below, ('tile', 'tm'), [(2 * i, 2 * i + 1) for i in last])  1.93 us
    ppermute x1, starting transfers between devices, local(): from_other = lax.ppermute(other, 'tile', other_pairs)  1.3 us
    ppermute x1, starting transfers between devices, local(): far_below = lax.ppermute(first[0], 'tile', [(i + 1, i) for i in last])  1.29 us
    ppermute x1, starting transfers between devices, local(): from_far = lax.ppermute(other, 'tile', [(i, i + 1) for i in last])  1.29 us
  transfers between devices with their start and end apart: 8, of which 2 were waited for; matrix products, arithmetic and copies ran while one was open for 0% of the time, Pallas kernels for 28%

profile of v3, /device:TPU:249, one launch (start us, length us, event | category | flops | bytes accessed | tf_op | source)
XLA Modules:
  0.0 24.3 jit_solution(15339122453159143767)
XLA Ops:
  0.0 2.2 %shard_map.73 = (bf16[4,8,6144]{2,1,0:T(8,128)(2,1)S(1)}, bf16[4,8,64,128]{3,2,1,0:T(8,128)(2,1)S(1)}, bf16[4,2,64,128]{3,2,1,0:T(8,128)(2,1)S(1)}, bf16[4,2,64,...) custom-call(bf16[4,8,6144]{2,1,0:T(8,128)(2,1)} %clip_hbm.1, ...), custom_call_target="tpu_custom_call" | custom-call | tf_op jit(solution)/shard_map/pallas_call | solution.py:262
  2.2 0.8 %collective-permute-start.3 = (bf16[4,8,64,128]{3,2,1,0:T(8,128)(2,1)S(1)}, bf16[4,8,64,128]{3,2,1,0:T(8,128)(2,1)S(1)}, u32[]{:S(2)}, u32[]{:S(2)}) collective-permute-start(bf16[4,8,64,128]{3,2,1,0:T(8,128)(2,1)S(1)} %get-tuple-element.37.refs_0_), channel_id=1, source_target_pairs={{0,1},{1,0},{2,3},{3,2},{4,5},{5,4},{6,7},{7,6},{8,9},{9,8},{10,11... | collective-permute-start | bytes 1572872 | tf_op jit(solution)/shard_map/ppermute | solution.py:275
  2.9 1.3 %collective-permute-start = (bf16[4,2,64,128]{3,2,1,0:T(8,128)(2,1)S(1)}, bf16[4,2,64,128]{3,2,1,0:T(8,128)(2,1)S(1)}, u32[]{:S(2)}, u32[]{:S(2)}) collective-permute-start(bf16[4,2,64,128]{3,2,1,0:T(8,128)(2,1)S(1)} %get-tuple-element.35), channel_id=1, source_target_pairs={{62,64},{126,128},{190,192},{63,65},{127,129},{191,193}} | collective-permute-start | bytes 393224 | tf_op jit(solution)/shard_map/ppermute | solution.py:272
  4.2 1.3 %collective-permute-start.2 = (bf16[4,2,64,128]{3,2,1,0:T(8,128)(2,1)S(1)}, bf16[4,2,64,128]{3,2,1,0:T(8,128)(2,1)S(1)}, u32[]{:S(2)}, u32[]{:S(2)}) collective-permute-start(bf16[4,2,64,128]{3,2,1,0:T(8,128)(2,1)S(1)} %get-tuple-element.35), channel_id=1, source_target_pairs={{0,64},{2,4},{4,2},{6,8},{8,6},{10,12},{12,10},{14,16},{16,14},{18... | collective-permute-start | bytes 393224 | tf_op jit(solution)/shard_map/ppermute | solution.py:274
  5.5 0.0 collective-permute-start.1
  6.2 0.0 collective-permute-done.3.refs_1_
  6.2 1.3 %collective-permute-start.6 = (bf16[4,2,64,128]{3,2,1,0:T(8,128)(2,1)S(1)}, bf16[4,2,64,128]{3,2,1,0:T(8,128)(2,1)S(1)}, u32[]{:S(2)}, u32[]{:S(2)}) collective-permute-start(bf16[4,2,64,128]{3,2,1,0:T(8,128)(2,1)S(1)} %get-tuple-element.57), channel_id=1, source_target_pairs={{64,62},{128,126},{192,190},{65,63},{129,127},{193,191}} | collective-permute-start | bytes 393224 | tf_op jit(solution)/shard_map/ppermute | solution.py:298
  7.5 0.0 copy-start
  7.5 6.7 %shard_map.75 = (bf16[2,2304,256]{2,1,0:T(8,128)(2,1)S(1)}, bf16[2,2304,256]{2,1,0:T(8,128)(2,1)S(1)}, f32[2,384,256]{2,1,0:T(8,128)S(1)}, f32[2,256,256]{2,1,0:T(8,128)S(1)}, f32[2,256,256]{2,1,0:T(8,128)S(1)}) custom-call(bf16[4,8,64,128]{3,2,1,0:T(8,128)(2,1)S(1)} %get-tuple-element, ...), custom_call_target="tpu_custom_call", output_to_operand_aliasing={{0}: (6, {}), {1}: (7, {}), {2}: (8, {}), {3}: (9, {}), {4}... | custom-call | tf_op jit(solution)/shard_map/pallas_call | solution.py:299
  14.2 0.0 collective-permute-done.other_far
  14.2 0.0 collective-permute-done.2.other
  14.2 0.0 collective-permute-done.1.near
  14.3 0.4 %collective-permute-start.4 = (bf16[4,2,64,128]{3,2,1,0:T(8,128)(2,1)S(1)}, bf16[4,2,64,128]{3,2,1,0:T(8,128)(2,1)S(1)}, u32[]{:S(2)}, u32[]{:S(2)}) collective-permute-start(bf16[4,2,64,128]{3,2,1,0:T(8,128)(2,1)S(1)} %get-tuple-element.55.above), channel_id=1, source_target_pairs={{0,1},{1,0},{2,3},{3,2},{4,5},{5,4},{6,7},{7,6},{8,9},{9,8},{10,11... | collective-permute-start | bytes 393224 | tf_op jit(solution)/shard_map/ppermute | solution.py:316
  14.7 0.2 collective-permute-start.5
  14.9 2.2 %collective-permute-done.6.far_below = bf16[4,2,64,128]{3,2,1,0:T(8,128)(2,1)S(1)} collective-permute-done((bf16[4,2,64,128]{3,2,1,0:T(8,128)(2,1)S(1)}, bf16[4,2,64,128]{3,2,1,0:T(8,128)(2,1)S(1)}, u32[]{:S(2)}, u32[]{:S(2)}) %collective-permute-start.6) | collective-permute-done | bytes 131104 | tf_op jit(solution)/shard_map/ppermute | solution.py:298
  17.1 1.3 %collective-permute-start.7 = (bf16[4,2,64,128]{3,2,1,0:T(8,128)(2,1)S(1)}, bf16[4,2,64,128]{3,2,1,0:T(8,128)(2,1)S(1)}, u32[]{:S(2)}, u32[]{:S(2)}) collective-permute-start(bf16[4,2,64,128]{3,2,1,0:T(8,128)(2,1)S(1)} %collective-permute-done.6.far_below), channel_id=1, source_target_pairs={{62,63},{126,127},{190,191}} | collective-permute-start | bytes 393224 | tf_op jit(solution)/shard_map/ppermute | solution.py:318
  18.4 0.0 collective-permute-done.4.early_above
  18.4 0.0 collective-permute-done.5.early_below
  18.4 1.9 %collective-permute-done.7.far_early_below = bf16[4,2,64,128]{3,2,1,0:T(8,128)(2,1)S(1)} collective-permute-done((bf16[4,2,64,128]{3,2,1,0:T(8,128)(2,1)S(1)}, bf16[4,2,64,128]{3,2,1,0:T(8,128)(2,1)S(1)}, u32[]{:S(2)}, u32[]{:S(2)}) %collective-permute-start.7) | collective-permute-done | bytes 131104 | tf_op jit(solution)/shard_map/ppermute | solution.py:318
  20.3 0.0 copy-done
  20.3 3.8 %shard_map.77 = bf16[4,8,6144]{2,1,0:T(8,128)(2,1)} custom-call(bf16[4,8,6144]{2,1,0:T(8,128)(2,1)S(1)} %get-tuple-element.34.clip, bf16[4,2,64,128]{3,2,1,0:T(8,128)(2,1)S(1)} %get-tuple-element.55.above, bf16[4,2,64,128]{3,2,1,0:T(8,128)(2,1)S(1)} %get-tuple-element.56.below, bf16[4,2,64,128]{3,2,1,0:T(8,128)(2,1)S(1)} %collective-permute-done.4.early_above, ...), custom_call_target="tpu_custom_call" | custom-call | tf_op jit(solution)/shard_map/pallas_call | solution.py:319
  (2 shorter events, 0.1 us)
Async XLA Ops:
  2.2 4.0 %collective-permute-start.3 = (bf16[4,8,64,128]{3,2,1,0:T(8,128)(2,1)S(1)}, bf16[4,8,64,128]{3,2,1,0:T(8,128)(2,1)S(1)}, u32[]{:S(2)}, u32[]{:S(2)}) collective-permute-start(bf16[4,8,64,128]{3,2,1,0:T(8,128)(2,1)S(1)} %get-tuple-element.37.refs_0_), channel_id=1, source_target_pairs={{0,1},{1,0},{2,3},{3,2},{4,5},{5,4},{6,7},{7,6},{8,9},{9,8},{10,11... | collective-permute-start | bytes 1572872 | tf_op jit(solution)/shard_map/ppermute | solution.py:275
  2.9 11.3 %collective-permute-start = (bf16[4,2,64,128]{3,2,1,0:T(8,128)(2,1)S(1)}, bf16[4,2,64,128]{3,2,1,0:T(8,128)(2,1)S(1)}, u32[]{:S(2)}, u32[]{:S(2)}) collective-permute-start(bf16[4,2,64,128]{3,2,1,0:T(8,128)(2,1)S(1)} %get-tuple-element.35), channel_id=1, source_target_pairs={{62,64},{126,128},{190,192},{63,65},{127,129},{191,193}} | collective-permute-start | bytes 393224 | tf_op jit(solution)/shard_map/ppermute | solution.py:272
  4.2 10.0 %collective-permute-start.2 = (bf16[4,2,64,128]{3,2,1,0:T(8,128)(2,1)S(1)}, bf16[4,2,64,128]{3,2,1,0:T(8,128)(2,1)S(1)}, u32[]{:S(2)}, u32[]{:S(2)}) collective-permute-start(bf16[4,2,64,128]{3,2,1,0:T(8,128)(2,1)S(1)} %get-tuple-element.35), channel_id=1, source_target_pairs={{0,64},{2,4},{4,2},{6,8},{8,6},{10,12},{12,10},{14,16},{16,14},{18... | collective-permute-start | bytes 393224 | tf_op jit(solution)/shard_map/ppermute | solution.py:274
  5.5 8.7 %collective-permute-start.1 = (bf16[4,2,64,128]{3,2,1,0:T(8,128)(2,1)S(1)}, bf16[4,2,64,128]{3,2,1,0:T(8,128)(2,1)S(1)}, u32[]{:S(2)}, u32[]{:S(2)}) collective-permute-start(bf16[4,2,64,128]{3,2,1,0:T(8,128)(2,1)S(1)} %get-tuple-element.36), channel_id=1, source_target_pairs={{0,2},{2,0},{4,6},{6,4},{8,10},{10,8},{12,14},{14,12},{16,18},{18,... | collective-permute-start | bytes 393224 | tf_op jit(solution)/shard_map/ppermute | solution.py:273
  6.2 10.9 %collective-permute-start.6 = (bf16[4,2,64,128]{3,2,1,0:T(8,128)(2,1)S(1)}, bf16[4,2,64,128]{3,2,1,0:T(8,128)(2,1)S(1)}, u32[]{:S(2)}, u32[]{:S(2)}) collective-permute-start(bf16[4,2,64,128]{3,2,1,0:T(8,128)(2,1)S(1)} %get-tuple-element.57), channel_id=1, source_target_pairs={{64,62},{128,126},{192,190},{65,63},{129,127},{193,191}} | collective-permute-start | bytes 393224 | tf_op jit(solution)/shard_map/ppermute | solution.py:298
  7.5 12.8 %copy-start = (s32[1,2]{1,0:T(1,128)S(1)}, s32[1,2]{1,0:T(1,128)}, u32[]{:S(2)}) copy-start(s32[1,2]{1,0:T(1,128)} %links.1) | copy-start | bytes 28
  14.3 4.1 %collective-permute-start.4 = (bf16[4,2,64,128]{3,2,1,0:T(8,128)(2,1)S(1)}, bf16[4,2,64,128]{3,2,1,0:T(8,128)(2,1)S(1)}, u32[]{:S(2)}, u32[]{:S(2)}) collective-permute-start(bf16[4,2,64,128]{3,2,1,0:T(8,128)(2,1)S(1)} %get-tuple-element.55.above), channel_id=1, source_target_pairs={{0,1},{1,0},{2,3},{3,2},{4,5},{5,4},{6,7},{7,6},{8,9},{9,8},{10,11... | collective-permute-start | bytes 393224 | tf_op jit(solution)/shard_map/ppermute | solution.py:316
  14.7 3.7 %collective-permute-start.5 = (bf16[4,2,64,128]{3,2,1,0:T(8,128)(2,1)S(1)}, bf16[4,2,64,128]{3,2,1,0:T(8,128)(2,1)S(1)}, u32[]{:S(2)}, u32[]{:S(2)}) collective-permute-start(bf16[4,2,64,128]{3,2,1,0:T(8,128)(2,1)S(1)} %get-tuple-element.56.below), channel_id=1, source_target_pairs={{0,1},{1,0},{2,3},{3,2},{4,5},{5,4},{6,7},{7,6},{8,9},{9,8},{10,11... | collective-permute-start | bytes 393224 | tf_op jit(solution)/shard_map/ppermute | solution.py:317
  17.1 3.2 %collective-permute-start.7 = (bf16[4,2,64,128]{3,2,1,0:T(8,128)(2,1)S(1)}, bf16[4,2,64,128]{3,2,1,0:T(8,128)(2,1)S(1)}, u32[]{:S(2)}, u32[]{:S(2)}) collective-permute-start(bf16[4,2,64,128]{3,2,1,0:T(8,128)(2,1)S(1)} %collective-permute-done.6.far_below), channel_id=1, source_target_pairs={{62,63},{126,127},{190,191}} | collective-permute-start | bytes 393224 | tf_op jit(solution)/shard_map/ppermute | solution.py:318

commit v4 on v3

v4 whole, which is shorter than its diff:
```python
import jax
import jax.numpy as jnp
from jax import lax
from jax.experimental import pallas as pl
from jax.experimental.pallas import tpu as pltpu
from jax.sharding import PartitionSpec as P

C = 96
L = 128
BW = 64
CORNER = 4
FAR = 32
STEP = BW + 8
BF = jnp.bfloat16
F32 = jnp.float32
VM = pltpu.VMEM
vmem = pl.BlockSpec(memory_space=pltpu.VMEM)
smem = pl.BlockSpec(memory_space=pltpu.SMEM)
hbm = pl.BlockSpec(memory_space=pltpu.HBM)
DMA = pltpu.SemaphoreType.DMA
PARAMS = pltpu.CompilerParams(vmem_limit_bytes=32 * 1024 * 1024)


def settle(x, half_gain):
    ms = jnp.sum(x * x, axis=-1, keepdims=True) * (1.0 / C)
    v = x * lax.rsqrt(ms + 1e-6) * half_gain
    return v + v * jnp.tanh(v)


def half_gain_of(gain):
    g = gain[...] * 0.5
    return jnp.concatenate([g, jnp.zeros((1, L - C), F32)], axis=1)


def spread(frame, scratch):
    pad = jnp.zeros((8, L - C), F32)
    for w in range(BW):
        piece = jnp.concatenate([frame[:, w * C : (w + 1) * C], pad], axis=1)
        scratch[pl.ds(w, 8, stride=STEP), :] = piece


def shifts(h):
    row = lax.broadcasted_iota(jnp.int32, (BW, 1), 0)
    left = jnp.where(row == 0, 0.0, pltpu.roll(h, 1, 0))
    right = jnp.where(row == BW - 1, 0.0, pltpu.roll(h, BW - 1, 0))
    return left.astype(BF), h.astype(BF), right.astype(BF)


def put(ref, t, r, h):
    for k, v in enumerate(shifts(h)):
        ref[k, t, r] = v


def pack_weights(weight, packed):
    zero = jnp.zeros((L, L), BF)
    for i in range(3):
        for k in range(3):
            blocks = []
            for j in range(3):
                w = weight[i, j, k * C : (k + 1) * C, :]
                w = jnp.concatenate([w, jnp.zeros((C, L - C), BF)], axis=1)
                blocks.append(jnp.concatenate([w, jnp.zeros((L - C, L), BF)], axis=0))
            for half in range(2):
                for a in range(2):
                    for b in range(2):
                        j = 2 * half + a - b
                        row = (i * 3 + k) * 256 + a * L
                        packed[half, row : row + L, b * L : (b + 1) * L] = blocks[j] if 0 <= j <= 2 else zero


def half_conv(field, frames, row, packed, half):
    pieces = []
    for i in range(3):
        for k in range(3):
            for a in range(2):
                pieces.append(field[k, i : i + frames, row + a].reshape(frames * BW, L))
    return jnp.dot(jnp.concatenate(pieces, axis=1), packed[half], preferred_element_type=F32)


def start(*copies):
    copies = [pltpu.make_async_copy(*copy) for copy in copies]
    for copy in copies:
        copy.start()
    return copies


def column_mask(widths):
    return (lax.broadcasted_iota(jnp.int32, (BW, L), 0) < widths[0]).astype(F32)


def masks_of(widths, links):
    mask = column_mask(widths)
    return mask, mask * links[0, 0].astype(F32), mask * links[0, 1].astype(F32)


def is_even():
    return lax.rem(lax.axis_index("tile"), 2) == 0


def is_first():
    return lax.rem(lax.axis_index("tile"), FAR) == 0


def send_kernel(
    clip_hbm, gain1_hbm, weight1_hbm, gain2_hbm, weight2_hbm,
    clip, hidden, bottom, near, top, weight1, gain2, weight2, gain1, scratch, sems,
):
    gain_copy = start((gain1_hbm, gain1, sems.at[4]))[0]
    frames = start(*((clip_hbm.at[t], clip.at[t], sems.at[t]) for t in range(4)))
    pairs = ((weight1_hbm, weight1), (gain2_hbm, gain2), (weight2_hbm, weight2))
    rest = start(*((src, dst, sems.at[5 + n]) for n, (src, dst) in enumerate(pairs)))
    gain_copy.wait()
    g = half_gain_of(gain1)
    even = is_even()
    ends = []
    for t in range(4):
        frames[t].wait()
        spread(clip[t].astype(F32), scratch.at[t])
        rows = [settle(scratch[t, r * STEP : r * STEP + BW, :], g) for r in range(8)]
        for r in range(8):
            hidden[t, r] = rows[r].astype(BF)
        ends += [rows]
    for half in range(2):
        first, last = (
            jnp.concatenate([ends[2 * half + t][r + n][:, :C] for t in range(2) for n in range(2)], axis=1)
            for r in (0, 6)
        )
        top[half] = first.astype(BF)
        bottom[half] = last.astype(BF)
        near[half] = jnp.where(even, last, first).astype(BF)
    for copy in rest:
        copy.wait()


def settle_pair(p, acc, g2, masks, x2):
    for t in range(6):
        for b in range(2):
            h = settle(acc[t * BW : (t + 1) * BW, b * L : (b + 1) * L], g2) * masks[t >= 2]
            put(x2, t, 2 * p - 2 + b, h)


def first_pair(p, x1, packed1):
    return half_conv(x1, 6, 2 * p - 2, packed1, 0) + half_conv(x1, 6, 2 * p, packed1, 1)


def both_masks(widths):
    mask = column_mask(widths)
    return mask * (lax.axis_index("tm") > 0).astype(F32), mask


def first_body(hidden, earlier, weight1, gain2, weight2, widths, packed1, packed2, part1, x1, x2):
    masks = both_masks(widths)
    g2 = half_gain_of(gain2)

    def fill(rows):
        for t in range(8):
            for r in rows:
                put(x1, t, r, (earlier if t < 4 else hidden)[t % 4, r].astype(F32) * masks[t >= 4])

    fill(range(4))
    pack_weights(weight1, packed1)
    acc1 = first_pair(1, x1, packed1)
    fill(range(4, 8))
    part1[0] = half_conv(x1, 6, 0, packed1, 1)
    settle_pair(1, acc1, g2, masks, x2)
    pack_weights(weight2, packed2)


def middle_body(gain2, widths, packed1, part1, x1, x2):
    masks = both_masks(widths)
    g2 = half_gain_of(gain2)
    acc2 = first_pair(2, x1, packed1)
    acc3 = first_pair(3, x1, packed1)
    settle_pair(2, acc2, g2, masks, x2)
    part1[1] = half_conv(x1, 6, 6, packed1, 0)
    settle_pair(3, acc3, g2, masks, x2)


def second_body(x2, packed2, part2, inner):
    for q in range(1, 3):
        inner[q - 1] = half_conv(x2, 4, 2 * q - 2, packed2, 0) + half_conv(x2, 4, 2 * q, packed2, 1)
    part2[0] = half_conv(x2, 4, 0, packed2, 1)
    part2[1] = half_conv(x2, 4, 4, packed2, 0)


def is_corner():
    return lax.rem(lax.axis_index("tile"), CORNER) == 0


def early_kernel(*refs):
    packed1, packed2, part1, x1, x2, part2, inner = refs[8:]

    @pl.when(is_corner())
    def _():
        first_body(*refs[:6], packed1, packed2, part1, x1, x2)

    @pl.when(is_first())
    def _():
        middle_body(refs[3], refs[5], packed1, part1, x1, x2)
        second_body(x2, packed2, part2, inner)


def first_kernel(*refs):
    packed1, packed2, part1, x1, x2 = refs[11:]

    @pl.when(jnp.logical_not(is_corner()))
    def _():
        first_body(*refs[:6], packed1, packed2, part1, x1, x2)

    @pl.when(jnp.logical_not(is_first()))
    def _():
        middle_body(refs[3], refs[5], packed1, part1, x1, x2)


def second_kernel(x2, packed2, part2_in, inner_in, part2, inner):
    @pl.when(jnp.logical_not(is_first()))
    def _():
        second_body(x2, packed2, part2, inner)


def post_kernel(
    clip, above, early_above, near, early_near, other, early_other, gain2, widths, links, packed1, packed2, part1, part2, inner,
    out_hbm, x1, x2, scratch, out, sems,
):
    g2 = half_gain_of(gain2)
    even = is_even()
    has_earlier = (lax.axis_index("tm") > 0).astype(F32)
    masks = masks_of(widths, links)
    early_masks = [m * has_earlier for m in masks]
    live = lax.broadcasted_iota(jnp.int32, (8, BW * C), 1) < widths[0] * C
    pad = jnp.zeros((BW, L - C), F32)
    for side in range(2):
        for half in range(4):
            pick = ((early_above, early_near, early_other), (above, near, other))[half // 2][side : side + 2]
            wide = jnp.where(even, *(rows[half % 2].astype(F32) for rows in pick))
            for n in range(4):
                h = jnp.concatenate([wide[:, n * C : (n + 1) * C], pad], axis=1)
                put(x1.at[side], 2 * half + n // 2, n % 2, h * (early_masks if half < 2 else masks)[1 + side])
        acc = part1[side] + half_conv(x1.at[side], 6, 0, packed1, side)
        for t in range(6):
            for b in range(2):
                m = (early_masks if t < 2 else masks)[1 + side if b == side else 0]
                put(x2.at[side], t, b, settle(acc[t * BW : (t + 1) * BW, b * L : (b + 1) * L], g2) * m)
    outer_rows = [part2[s] + half_conv(x2.at[s], 4, 0, packed2, s) for s in range(2)]
    copies = []
    for t in range(4):
        for q in range(4):
            acc = inner[q - 1] if q in (1, 2) else outer_rows[q // 3]
            for b in range(2):
                r = 2 * q + b
                scratch[t, r * STEP : r * STEP + BW, :] = acc[t * BW : (t + 1) * BW, b * L : (b + 1) * L]
        pieces = [scratch[t, pl.ds(w, 8, stride=STEP), :][:, :C] for w in range(BW)]
        y = clip[t].astype(F32) + jnp.concatenate(pieces, axis=1)
        out[t] = jnp.where(live, y, 0.0).astype(BF)
        copies += start((out.at[t], out_hbm.at[t], sems.at[t]))
    for copy in copies:
        copy.wait()


def local(clip, gain1, weight1, gain2, weight2, widths, links):
    tiles = lax.axis_size("tile")
    near_pairs = [(i, i ^ 1) for i in range(tiles)]
    odd_pairs = [(i + 1, i) for i in range(1, tiles - 1, 2)]
    cores = [(0, 1), (1, 0)]
    gain1, gain2 = gain1.reshape(1, C), gain2.reshape(1, C)
    clip, gain1, weight1, gain2, weight2 = (
        pltpu.with_memory_space_constraint(x, pltpu.HBM) for x in (clip, gain1, weight1, gain2, weight2)
    )
    edge = VM((2, BW, 4 * C), BF)
    weight = VM((3, 3, 3 * C, C), BF)
    clip, hidden, bottom, near, top, weight1, gain2, weight2 = pl.pallas_call(
        send_kernel,
        out_shape=(
            VM((4, 8, BW * C), BF), VM((4, 8, BW, L), BF), edge, edge, edge, weight, VM((1, C), F32), weight,
        ),
        in_specs=[hbm] * 5,
        out_specs=(vmem,) * 8,
        scratch_shapes=[VM((1, C), F32), VM((4, 8 * STEP, L), F32), DMA((8,))],
        compiler_params=PARAMS,
    )(clip, gain1, weight1, gain2, weight2)
    turn = tiles - FAR // 2
    ups = {i: i + 1 for i in range(tiles)} | {turn: 0, tiles - 1: turn + 1}
    above = lax.ppermute(bottom, "tile", list(ups.items()))
    near = lax.ppermute(near, "tile", near_pairs)
    earlier = lax.ppermute(hidden, "tm", cores)
    state = (
        VM((2, 9 * 256, 256), BF),
        VM((2, 9 * 256, 256), BF),
        VM((2, 6 * BW, 256), F32),
        VM((3, 8, 8, BW, L), BF),
        VM((3, 6, 6, BW, L), BF),
        VM((2, 4 * BW, 256), F32),
        VM((2, 4 * BW, 256), F32),
    )
    inputs = (hidden, earlier, weight1, gain2, weight2, widths)
    specs = [vmem] * 5 + [smem]
    top, *made = pl.pallas_call(
        early_kernel,
        out_shape=(edge, *state),
        in_specs=specs + [vmem],
        out_specs=(vmem,) * 8,
        input_output_aliases={6: 0},
        compiler_params=PARAMS,
    )(*inputs, top)
    other = lax.ppermute(top, "tile", odd_pairs)
    packed1, packed2, part1, _, x2 = pl.pallas_call(
        first_kernel,
        out_shape=state[:5],
        in_specs=specs + [vmem] * 5,
        out_specs=(vmem,) * 5,
        input_output_aliases={6 + n: n for n in range(5)},
        compiler_params=PARAMS,
    )(*inputs, *made[:5])
    above, near, x2 = lax.optimization_barrier((above, near, x2))
    early_above = lax.ppermute(above, "tm", cores)
    early_near = lax.ppermute(near, "tm", cores)
    part2, inner = pl.pallas_call(
        second_kernel,
        out_shape=state[5:],
        in_specs=[vmem] * 4,
        out_specs=(vmem,) * 2,
        input_output_aliases={2: 0, 3: 1},
        compiler_params=PARAMS,
    )(x2, packed2, *made[5:])
    other, part2 = lax.optimization_barrier((other, part2))
    early_other = lax.ppermute(other, ("tile", "tm"), [(2 * i, 2 * i + 1) for i in range(1, tiles, 2)])
    return pl.pallas_call(
        post_kernel,
        out_shape=pltpu.HBM((4, 8, BW * C), BF),
        in_specs=[vmem] * 8 + [smem, smem] + [vmem] * 5,
        out_specs=hbm,
        scratch_shapes=[
            VM((2, 3, 8, 2, BW, L), BF),
            VM((2, 3, 6, 2, BW, L), BF),
            VM((4, 8 * STEP, L), F32),
            VM((4, 8, BW * C), BF),
            DMA((4,)),
        ],
        compiler_params=PARAMS,
    )(
        clip, above, early_above, near, early_near, other, early_other, gain2, widths, links,
        packed1, packed2, part1, part2, inner,
    )


def solution(mesh):
    in_specs = (P("tm", "tile", None), P(), P(), P(), P(), P("tile"), P("tile", None))
    out_specs = P("tm", "tile", None)
    return jax.shard_map(local, mesh=mesh, in_specs=in_specs, out_specs=out_specs, check_vma=False)
```

time: 24.4 us -> 23 us (0.943)
  the two profiles are of different devices: /device:TPU:249 before, /device:TPU:6 now
where the time goes in v4:
time: 23 us; the launch traced here: 22.6 us
  Pallas kernels  13.7 us (60%)
  starting transfers between devices  6.6 us (29%)
  waiting for transfers between devices  1.37 us (6%)
  between operations  0.93 us (4%)
    pallas_call x1, Pallas kernels, local(): pl.pallas_call(early_kernel, out_shape=(edge, *state), in_specs=specs + [...  7.34 us
    pallas_call x1, Pallas kernels, local(): pl.pallas_call(post_kernel, out_shape=pltpu.HBM((4, 8, BW * C), BF), in_s...  3.93 us
    pallas_call x1, Pallas kernels, local(): pl.pallas_call(send_kernel, out_shape=(VM((4, 8, BW * C), BF), VM((4, 8,...  2.21 us
    ppermute x1, starting transfers between devices, local(): other = lax.ppermute(top, 'tile', odd_pairs)  2.04 us
    ppermute x1, starting transfers between devices, local(): above = lax.ppermute(bottom, 'tile', list(ups.items()))  1.65 us
    ppermute x1, starting transfers between devices, local(): near = lax.ppermute(near, 'tile', near_pairs)  1.58 us
    ppermute x1, waiting for transfers between devices, local(): other = lax.ppermute(top, 'tile', odd_pairs)  1.35 us
    ppermute x1, starting transfers between devices, local(): lax.ppermute(other, ('tile', 'tm'), [(2 * i, 2 * i + 1) for i in range(1,...  0.65 us
  transfers between devices with their start and end apart: 7, of which 1 were waited for; matrix products, arithmetic and copies ran while one was open for 0% of the time, Pallas kernels for 33%

profile of v4, /device:TPU:6, one launch (start us, length us, event | category | flops | bytes accessed | tf_op | source)
XLA Modules:
  0.0 22.6 jit_solution(4393041775096183205)
XLA Ops:
  0.0 2.2 %shard_map.73 = (bf16[4,8,6144]{2,1,0:T(8,128)(2,1)S(1)}, bf16[4,8,64,128]{3,2,1,0:T(8,128)(2,1)S(1)}, bf16[2,64,384]{2,1,0:T(8,128)(2,1)S(1)}, bf16[2,64,384]{2...) custom-call(bf16[4,8,6144]{2,1,0:T(8,128)(2,1)} %clip_hbm.1, ...), custom_call_target="tpu_custom_call" | custom-call | tf_op jit(solution)/shard_map/pallas_call | solution.py:271
  2.2 0.1 collective-permute-start.2
  2.3 1.7 %collective-permute-start = (bf16[2,64,384]{2,1,0:T(8,128)(2,1)S(1)}, bf16[2,64,384]{2,1,0:T(8,128)(2,1)S(1)}, u32[]{:S(2)}, u32[]{:S(2)}) collective-permute-start(bf16[2,64,384]{2,1,0:T(8,128)(2,1)S(1)} %get-tuple-element.33), channel_id=1, source_target_pairs={{0,2},{2,4},{4,6},{6,8},{8,10},{10,12},{12,14},{14,16},{16,18},{18... | collective-permute-start | bytes 294920 | tf_op jit(solution)/shard_map/ppermute | solution.py:283
  4.0 1.6 %collective-permute-start.1 = (bf16[2,64,384]{2,1,0:T(8,128)(2,1)S(1)}, bf16[2,64,384]{2,1,0:T(8,128)(2,1)S(1)}, u32[]{:S(2)}, u32[]{:S(2)}) collective-permute-start(bf16[2,64,384]{2,1,0:T(8,128)(2,1)S(1)} %get-tuple-element.34), channel_id=1, source_target_pairs={{0,2},{2,0},{4,6},{6,4},{8,10},{10,8},{12,14},{14,12},{16,18},{18,... | collective-permute-start | bytes 294920 | tf_op jit(solution)/shard_map/ppermute | solution.py:284
  6.2 0.0 collective-permute-done.2.refs_1_
  6.2 7.3 %shard_map.74 = (bf16[2,64,384]{2,1,0:T(8,128)(2,1)S(1)}, bf16[2,2304,256]{2,1,0:T(8,128)(2,1)S(1)}, bf16[2,2304,256]{2,1,0:T(8,128)(2,1)S(1)}, f32[2,384,256]{2...) custom-call(bf16[4,8,64,128]{3,2,1,0:T(8,128)(2,1)S(1)} %get-tuple-e, ...), custom_call_target="tpu_custom_call", output_to_operand_aliasing={{0}: (6, {})} | custom-call | tf_op jit(solution)/shard_map/pallas_call | solution.py:297
  13.6 2.0 %collective-permute-start.5 = (bf16[2,64,384]{2,1,0:T(8,128)(2,1)S(1)}, bf16[2,64,384]{2,1,0:T(8,128)(2,1)S(1)}, u32[]{:S(2)}, u32[]{:S(2)}) collective-permute-start(bf16[2,64,384]{2,1,0:T(8,128)(2,1)S(1)} %get-tuple-element.48), channel_id=1, source_target_pairs={{4,2},{8,6},{12,10},{16,14},{20,18},{24,22},{28,26},{32,30},{36,34... | collective-permute-start | bytes 294920 | tf_op jit(solution)/shard_map/ppermute | solution.py:305
  15.6 0.2 shard_map.75
  15.8 0.0 collective-permute-done.above
  15.8 0.0 collective-permute-done.1.near
  15.8 0.1 collective-permute-start.3
  15.9 0.5 %collective-permute-start.4 = (bf16[2,64,384]{2,1,0:T(8,128)(2,1)S(1)}, bf16[2,64,384]{2,1,0:T(8,128)(2,1)S(1)}, u32[]{:S(2)}, u32[]{:S(2)}) collective-permute-start(bf16[2,64,384]{2,1,0:T(8,128)(2,1)S(1)} %collective-permute-done.1.near), channel_id=1, source_target_pairs={{0,1},{1,0},{2,3},{3,2},{4,5},{5,4},{6,7},{7,6},{8,9},{9,8},{10,11... | collective-permute-start | bytes 294920 | tf_op jit(solution)/shard_map/ppermute | solution.py:316
  16.4 0.0 copy-start
  16.4 1.4 %collective-permute-done.5.other = bf16[2,64,384]{2,1,0:T(8,128)(2,1)S(1)} collective-permute-done((bf16[2,64,384]{2,1,0:T(8,128)(2,1)S(1)}, bf16[2,64,384]{2,1,0:T(8,128)(2,1)S(1)}, u32[]{:S(2)}, u32[]{:S(2)}) %collective-permute-start.5) | collective-permute-done | bytes 98336 | tf_op jit(solution)/shard_map/ppermute | solution.py:305
  17.8 0.7 %collective-permute-start.6 = (bf16[2,64,384]{2,1,0:T(8,128)(2,1)S(1)}, bf16[2,64,384]{2,1,0:T(8,128)(2,1)S(1)}, u32[]{:S(2)}, u32[]{:S(2)}) collective-permute-start(bf16[2,64,384]{2,1,0:T(8,128)(2,1)S(1)} %collective-permute-done.5.other), channel_id=1, source_target_pairs={{2,3},{6,7},{10,11},{14,15},{18,19},{22,23},{26,27},{30,31},{34,35... | collective-permute-start | bytes 294920 | tf_op jit(solution)/shard_map/ppermute | solution.py:326
  18.5 0.0 collective-permute-done.3.early_above
  18.5 0.0 collective-permute-done.4.early_near
  18.5 0.0 collective-permute-done.6.early_other
  18.5 0.0 copy-done
  18.5 3.9 %shard_map.77 = bf16[4,8,6144]{2,1,0:T(8,128)(2,1)} custom-call(bf16[4,8,6144]{2,1,0:T(8,128)(2,1)S(1)} %get-tuple-element.32.clip, bf16[2,64,384]{2,1,0:T(8,128)(2,1)S(1)} %collective-permute-done.above, bf16[2,64,384]{2,1,0:T(8,128)(2,1)S(1)} %collective-permute-done.3.early_above, bf16[2,64,384]{2,1,0:T(8,128)(2,1)S(1)} %collective-permute-done.1.near, ...), custom_call_target="tpu_custom_call" | custom-call | tf_op jit(solution)/shard_map/pallas_call | solution.py:327
  (1 shorter events, 0.0 us)
Async XLA Ops:
  2.2 4.0 %collective-permute-start.2 = (bf16[4,8,64,128]{3,2,1,0:T(8,128)(2,1)S(1)}, bf16[4,8,64,128]{3,2,1,0:T(8,128)(2,1)S(1)}, u32[]{:S(2)}, u32[]{:S(2)}) collective-permute-start(bf16[4,8,64,128]{3,2,1,0:T(8,128)(2,1)S(1)} %get-tuple-element.35.refs_0_), channel_id=1, source_target_pairs={{0,1},{1,0},{2,3},{3,2},{4,5},{5,4},{6,7},{7,6},{8,9},{9,8},{10,11... | collective-permute-start | bytes 1572872 | tf_op jit(solution)/shard_map/ppermute | solution.py:285
  2.3 13.5 %collective-permute-start = (bf16[2,64,384]{2,1,0:T(8,128)(2,1)S(1)}, bf16[2,64,384]{2,1,0:T(8,128)(2,1)S(1)}, u32[]{:S(2)}, u32[]{:S(2)}) collective-permute-start(bf16[2,64,384]{2,1,0:T(8,128)(2,1)S(1)} %get-tuple-element.33), channel_id=1, source_target_pairs={{0,2},{2,4},{4,6},{6,8},{8,10},{10,12},{12,14},{14,16},{16,18},{18... | collective-permute-start | bytes 294920 | tf_op jit(solution)/shard_map/ppermute | solution.py:283
  4.0 11.9 %collective-permute-start.1 = (bf16[2,64,384]{2,1,0:T(8,128)(2,1)S(1)}, bf16[2,64,384]{2,1,0:T(8,128)(2,1)S(1)}, u32[]{:S(2)}, u32[]{:S(2)}) collective-permute-start(bf16[2,64,384]{2,1,0:T(8,128)(2,1)S(1)} %get-tuple-element.34), channel_id=1, source_target_pairs={{0,2},{2,0},{4,6},{6,4},{8,10},{10,8},{12,14},{14,12},{16,18},{18,... | collective-permute-start | bytes 294920 | tf_op jit(solution)/shard_map/ppermute | solution.py:284
  13.6 4.2 %collective-permute-start.5 = (bf16[2,64,384]{2,1,0:T(8,128)(2,1)S(1)}, bf16[2,64,384]{2,1,0:T(8,128)(2,1)S(1)}, u32[]{:S(2)}, u32[]{:S(2)}) collective-permute-start(bf16[2,64,384]{2,1,0:T(8,128)(2,1)S(1)} %get-tuple-element.48), channel_id=1, source_target_pairs={{4,2},{8,6},{12,10},{16,14},{20,18},{24,22},{28,26},{32,30},{36,34... | collective-permute-start | bytes 294920 | tf_op jit(solution)/shard_map/ppermute | solution.py:305
  15.8 2.6 %collective-permute-start.3 = (bf16[2,64,384]{2,1,0:T(8,128)(2,1)S(1)}, bf16[2,64,384]{2,1,0:T(8,128)(2,1)S(1)}, u32[]{:S(2)}, u32[]{:S(2)}) collective-permute-start(bf16[2,64,384]{2,1,0:T(8,128)(2,1)S(1)} %collective-permute-done.above), channel_id=1, source_target_pairs={{0,1},{1,0},{2,3},{3,2},{4,5},{5,4},{6,7},{7,6},{8,9},{9,8},{10,11... | collective-permute-start | bytes 294920 | tf_op jit(solution)/shard_map/ppermute | solution.py:315
  15.9 2.5 %collective-permute-start.4 = (bf16[2,64,384]{2,1,0:T(8,128)(2,1)S(1)}, bf16[2,64,384]{2,1,0:T(8,128)(2,1)S(1)}, u32[]{:S(2)}, u32[]{:S(2)}) collective-permute-start(bf16[2,64,384]{2,1,0:T(8,128)(2,1)S(1)} %collective-permute-done.1.near), channel_id=1, source_target_pairs={{0,1},{1,0},{2,3},{3,2},{4,5},{5,4},{6,7},{7,6},{8,9},{9,8},{10,11... | collective-permute-start | bytes 294920 | tf_op jit(solution)/shard_map/ppermute | solution.py:316
  16.4 2.1 %copy-start = (s32[1,2]{1,0:T(1,128)S(1)}, s32[1,2]{1,0:T(1,128)}, u32[]{:S(2)}) copy-start(s32[1,2]{1,0:T(1,128)} %links.1) | copy-start | bytes 28
  17.8 0.7 %collective-permute-start.6 = (bf16[2,64,384]{2,1,0:T(8,128)(2,1)S(1)}, bf16[2,64,384]{2,1,0:T(8,128)(2,1)S(1)}, u32[]{:S(2)}, u32[]{:S(2)}) collective-permute-start(bf16[2,64,384]{2,1,0:T(8,128)(2,1)S(1)} %collective-permute-done.5.other), channel_id=1, source_target_pairs={{2,3},{6,7},{10,11},{14,15},{18,19},{22,23},{26,27},{30,31},{34,35... | collective-permute-start | bytes 294920 | tf_op jit(solution)/shard_map/ppermute | solution.py:326

commit v5 on v4

--- a/solution.py
+++ b/solution.py
@@ -18,6 +18,8 @@
 smem = pl.BlockSpec(memory_space=pltpu.SMEM)
 hbm = pl.BlockSpec(memory_space=pltpu.HBM)
 DMA = pltpu.SemaphoreType.DMA
+SMALL = pl.CostEstimate(flops=1, bytes_accessed=1, transcendentals=0)
+LARGE = pl.CostEstimate(flops=10**10, bytes_accessed=10**7, transcendentals=10**6)
 PARAMS = pltpu.CompilerParams(vmem_limit_bytes=32 * 1024 * 1024)
 
 
@@ -90,7 +92,7 @@
 
 def masks_of(widths, links):
     mask = column_mask(widths)
-    return mask, mask * links[0, 0].astype(F32), mask * links[0, 1].astype(F32)
+    return mask, mask * links[:, 0:1].astype(F32), mask * links[:, 1:2].astype(F32)
 
 
 def is_even():
@@ -218,21 +220,18 @@
         second_body(x2, packed2, part2, inner)
 
 
-def post_kernel(
-    clip, above, early_above, near, early_near, other, early_other, gain2, widths, links, packed1, packed2, part1, part2, inner,
-    out_hbm, x1, x2, scratch, out, sems,
+def post_body(
+    ends, clip, gain2, widths, links, packed1, packed2, part1, part2, inner, out_hbm, x1, x2, scratch, out, sems
 ):
     g2 = half_gain_of(gain2)
-    even = is_even()
+    masks = masks_of(widths, links)
     has_earlier = (lax.axis_index("tm") > 0).astype(F32)
-    masks = masks_of(widths, links)
     early_masks = [m * has_earlier for m in masks]
     live = lax.broadcasted_iota(jnp.int32, (8, BW * C), 1) < widths[0] * C
     pad = jnp.zeros((BW, L - C), F32)
     for side in range(2):
         for half in range(4):
-            pick = ((early_above, early_near, early_other), (above, near, other))[half // 2][side : side + 2]
-            wide = jnp.where(even, *(rows[half % 2].astype(F32) for rows in pick))
+            wide = ends[side][half // 2][half % 2][...].astype(F32)
             for n in range(4):
                 h = jnp.concatenate([wide[:, n * C : (n + 1) * C], pad], axis=1)
                 put(x1.at[side], 2 * half + n // 2, n % 2, h * (early_masks if half < 2 else masks)[1 + side])
@@ -241,11 +240,10 @@
             for b in range(2):
                 m = (early_masks if t < 2 else masks)[1 + side if b == side else 0]
                 put(x2.at[side], t, b, settle(acc[t * BW : (t + 1) * BW, b * L : (b + 1) * L], g2) * m)
-    outer_rows = [part2[s] + half_conv(x2.at[s], 4, 0, packed2, s) for s in range(2)]
+    outer = [part2[s] + half_conv(x2.at[s], 4, 0, packed2, s) for s in range(2)]
     copies = []
     for t in range(4):
-        for q in range(4):
-            acc = inner[q - 1] if q in (1, 2) else outer_rows[q // 3]
+        for q, acc in enumerate((outer[0], inner.at[0], inner.at[1], outer[1])):
             for b in range(2):
                 r = 2 * q + b
                 scratch[t, r * STEP : r * STEP + BW, :] = acc[t * BW : (t + 1) * BW, b * L : (b + 1) * L]
@@ -255,6 +253,24 @@
         copies += start((out.at[t], out_hbm.at[t], sems.at[t]))
     for copy in copies:
         copy.wait()
+
+
+def split_kernel(above, near, *halves):
+    for n in range(2):
+        halves[n][...] = above[n]
+        halves[2 + n][...] = near[n]
+
+
+def even_kernel(*refs):
+    @pl.when(is_even())
+    def _():
+        post_body(((refs[:2], refs[2:4]), (refs[4:6], refs[6:8])), *refs[8:])
+
+
+def odd_kernel(*refs):
+    @pl.when(jnp.logical_not(is_even()))
+    def _():
+        post_body(((refs[:2], refs[2:4]), refs[4:6]), *refs[7:])
 
 
 def local(clip, gain1, weight1, gain2, weight2, widths, links):
@@ -312,35 +328,56 @@
         compiler_params=PARAMS,
     )(*inputs, *made[:5])
     above, near, x2 = lax.optimization_barrier((above, near, x2))
-    early_above = lax.ppermute(above, "tm", cores)
-    early_near = lax.ppermute(near, "tm", cores)
+    half = VM((BW, 4 * C), BF)
+    halves = pl.pallas_call(
+        split_kernel,
+        out_shape=(half,) * 4,
+        in_specs=[vmem] * 2,
+        out_specs=(vmem,) * 4,
+        cost_estimate=SMALL,
+        compiler_params=PARAMS,
+    )(above, near)
+    early_halves = [lax.ppermute(x, "tm", cores) for x in halves]
+    above = (*early_halves[:2], *halves[:2])
+    near = (*early_halves[2:], *halves[2:])
     part2, inner = pl.pallas_call(
         second_kernel,
         out_shape=state[5:],
         in_specs=[vmem] * 4,
         out_specs=(vmem,) * 2,
         input_output_aliases={2: 0, 3: 1},
+        cost_estimate=SMALL,
         compiler_params=PARAMS,
     )(x2, packed2, *made[5:])
-    other, part2 = lax.optimization_barrier((other, part2))
-    early_other = lax.ppermute(other, ("tile", "tm"), [(2 * i, 2 * i + 1) for i in range(1, tiles, 2)])
+    early_other = lax.ppermute(other, "tm", cores)
+    inputs = (clip, gain2, widths, links, packed1, packed2, part1, part2, inner)
+    specs = [vmem] * 2 + [smem] + [vmem] * 6
+    out = pltpu.HBM((4, 8, BW * C), BF)
+    scratch = [
+        VM((2, 3, 8, 2, BW, L), BF),
+        VM((2, 3, 6, 2, BW, L), BF),
+        VM((4, 8 * STEP, L), F32),
+        VM((4, 8, BW * C), BF),
+        DMA((4,)),
+    ]
+    done = pl.pallas_call(
+        even_kernel,
+        out_shape=out,
+        in_specs=[vmem] * 8 + specs,
+        out_specs=hbm,
+        scratch_shapes=scratch,
+        cost_estimate=LARGE,
+        compiler_params=PARAMS,
+    )(*above, *near, *inputs)
     return pl.pallas_call(
-        post_kernel,
-        out_shape=pltpu.HBM((4, 8, BW * C), BF),
-        in_specs=[vmem] * 8 + [smem, smem] + [vmem] * 5,
+        odd_kernel,
+        out_shape=out,
+        in_specs=[vmem] * 6 + [hbm] + specs,
         out_specs=hbm,
-        scratch_shapes=[
-            VM((2, 3, 8, 2, BW, L), BF),
-            VM((2, 3, 6, 2, BW, L), BF),
-            VM((4, 8 * STEP, L), F32),
-            VM((4, 8, BW * C), BF),
-            DMA((4,)),
-        ],
-        compiler_params=PARAMS,
-    )(
-        clip, above, early_above, near, early_near, other, early_other, gain2, widths, links,
-        packed1, packed2, part1, part2, inner,
-    )
+        scratch_shapes=scratch,
+        input_output_aliases={6: 0},
+        compiler_params=PARAMS,
+    )(*near, early_other, other, done, *inputs)
 
 
 def solution(mesh):

time: 23 us -> 22.5 us (0.978)
  the two profiles are of different devices: /device:TPU:6 before, /device:TPU:1 now
where the time goes in v5:
time: 22.5 us; the launch traced here: 22.3 us
  Pallas kernels  13.3 us (59%)
  starting transfers between devices  6.84 us (30%)
  waiting for transfers between devices  1.33 us (6%)
  between operations  0.88 us (4%)
    pallas_call x1, Pallas kernels, local(): pl.pallas_call(early_kernel, out_shape=(edge, *state), in_specs=specs + [...  7.34 us
    pallas_call x1, Pallas kernels, local(): pl.pallas_call(even_kernel, out_shape=out, in_specs=[vmem] * 8 + specs, o...  3.45 us
    ppermute x1, starting transfers between devices, local(): earlier = lax.ppermute(hidden, 'tm', cores)  3.33 us
    pallas_call x1, Pallas kernels, local(): pl.pallas_call(send_kernel, out_shape=(VM((4, 8, BW * C), BF), VM((4, 8,...  2.21 us
    ppermute x4, starting transfers between devices, local(): early_halves = [lax.ppermute(x, 'tm', cores) for x in halves]  1.56 us
    ppermute x1, starting transfers between devices, local(): near = lax.ppermute(near, 'tile', near_pairs)  0.87 us
    ppermute x4, waiting for transfers between devices, local(): early_halves = [lax.ppermute(x, 'tm', cores) for x in halves]  0.71 us
    ppermute x1, starting transfers between devices, local(): other = lax.ppermute(top, 'tile', odd_pairs)  0.67 us
  transfers between devices with their start and end apart: 9, of which 4 were waited for; matrix products, arithmetic and copies ran while one was open for 0% of the time, Pallas kernels for 49%

profile of v5, /device:TPU:1, one launch (start us, length us, event | category | flops | bytes accessed | tf_op | source)
XLA Modules:
  0.0 22.3 jit_solution(9036223270862732469)
XLA Ops:
  0.0 2.2 %shard_map.73 = (bf16[4,8,6144]{2,1,0:T(8,128)(2,1)S(1)}, bf16[4,8,64,128]{3,2,1,0:T(8,128)(2,1)S(1)}, bf16[2,64,384]{2,1,0:T(8,128)(2,1)S(1)}, bf16[2,64,384]{2...) custom-call(bf16[4,8,6144]{2,1,0:T(8,128)(2,1)} %clip_hbm.1, ...), custom_call_target="tpu_custom_call" | custom-call | tf_op jit(solution)/shard_map/pallas_call | solution.py:287
  2.2 3.3 %collective-permute-start.2 = (bf16[4,8,64,128]{3,2,1,0:T(8,128)(2,1)S(1)}, bf16[4,8,64,128]{3,2,1,0:T(8,128)(2,1)S(1)}, u32[]{:S(2)}, u32[]{:S(2)}) collective-permute-start(bf16[4,8,64,128]{3,2,1,0:T(8,128)(2,1)S(1)} %get-tuple-element.36.refs_0_), channel_id=1, source_target_pairs={{0,1},{1,0},{2,3},{3,2},{4,5},{5,4},{6,7},{7,6},{8,9},{9,8},{10,11... | collective-permute-start | bytes 1572872 | tf_op jit(solution)/shard_map/ppermute | solution.py:301
  5.5 0.0 collective-permute-start
  5.5 0.9 %collective-permute-start.1 = (bf16[2,64,384]{2,1,0:T(8,128)(2,1)S(1)}, bf16[2,64,384]{2,1,0:T(8,128)(2,1)S(1)}, u32[]{:S(2)}, u32[]{:S(2)}) collective-permute-start(bf16[2,64,384]{2,1,0:T(8,128)(2,1)S(1)} %get-tuple-element.35), channel_id=1, source_target_pairs={{0,2},{2,0},{4,6},{6,4},{8,10},{10,8},{12,14},{14,12},{16,18},{18,... | collective-permute-start | bytes 294920 | tf_op jit(solution)/shard_map/ppermute | solution.py:300
  7.1 0.0 collective-permute-done.2.refs_1_
  7.1 7.3 %shard_map.74 = (bf16[2,64,384]{2,1,0:T(8,128)(2,1)S(1)}, bf16[2,2304,256]{2,1,0:T(8,128)(2,1)S(1)}, bf16[2,2304,256]{2,1,0:T(8,128)(2,1)S(1)}, f32[2,384,256]{2...) custom-call(bf16[4,8,64,128]{3,2,1,0:T(8,128)(2,1)S(1)} %get-tuple-e, ...), custom_call_target="tpu_custom_call", output_to_operand_aliasing={{0}: (6, {})} | custom-call | tf_op jit(solution)/shard_map/pallas_call | solution.py:313
  14.4 0.7 %collective-permute-start.5 = (bf16[2,64,384]{2,1,0:T(8,128)(2,1)S(1)}, bf16[2,64,384]{2,1,0:T(8,128)(2,1)S(1)}, u32[]{:S(2)}, u32[]{:S(2)}) collective-permute-start(bf16[2,64,384]{2,1,0:T(8,128)(2,1)S(1)} %get-tuple-element.51), channel_id=1, source_target_pairs={{4,2},{8,6},{12,10},{16,14},{20,18},{24,22},{28,26},{32,30},{36,34... | collective-permute-start | bytes 294920 | tf_op jit(solution)/shard_map/ppermute | solution.py:321
  15.1 0.2 shard_map.75
  15.3 0.6 %collective-permute-done.above = bf16[2,64,384]{2,1,0:T(8,128)(2,1)S(1)} collective-permute-done((bf16[2,64,384]{2,1,0:T(8,128)(2,1)S(1)}, bf16[2,64,384]{2,1,0:T(8,128)(2,1)S(1)}, u32[]{:S(2)}, u32[]{:S(2)}) %collective-permute-start) | collective-permute-done | bytes 98336 | tf_op jit(solution)/shard_map/ppermute | solution.py:299
  15.9 0.0 collective-permute-done.1.near
  15.9 1.0 %collective-permute-start.7 = (bf16[64,384]{1,0:T(8,128)(2,1)S(1)}, bf16[64,384]{1,0:T(8,128)(2,1)S(1)}, u32[]{:S(2)}, u32[]{:S(2)}) collective-permute-start(bf16[64,384]{1,0:T(8,128)(2,1)S(1)} %get-tuple-element.52.refs_2_), channel_id=1, source_target_pairs={{0,1},{1,0},{2,3},{3,2},{4,5},{5,4},{6,7},{7,6},{8,9},{9,8},{10,11... | collective-permute-start | bytes 147464 | tf_op jit(solution)/shard_map/ppermute | solution.py:340
  16.9 0.1 collective-permute-start.8
  17.0 0.4 %collective-permute-start.3 = (bf16[64,384]{1,0:T(8,128)(2,1)S(1)}, bf16[64,384]{1,0:T(8,128)(2,1)S(1)}, u32[]{:S(2)}, u32[]{:S(2)}) collective-permute-start(bf16[64,384]{1,0:T(8,128)(2,1)S(1)} %get-tuple-element.49.refs_6_.refs_2_), channel_id=1, source_target_pairs={{0,1},{1,0},{2,3},{3,2},{4,5},{5,4},{6,7},{7,6},{8,9},{9,8},{10,11... | collective-permute-start | bytes 147464 | tf_op jit(solution)/shard_map/ppermute | solution.py:340
  17.4 0.1 collective-permute-start.4
  17.5 0.0 copy-start
  17.5 0.0 collective-permute-done.5.refs_5_
  17.5 0.4 %collective-permute-start.6 = (bf16[2,64,384]{2,1,0:T(8,128)(2,1)S(1)}, bf16[2,64,384]{2,1,0:T(8,128)(2,1)S(1)}, u32[]{:S(2)}, u32[]{:S(2)}) collective-permute-start(bf16[2,64,384]{2,1,0:T(8,128)(2,1)S(1)} %collective-permute-done.5.refs_5_), channel_id=1, source_target_pairs={{0,1},{1,0},{2,3},{3,2},{4,5},{5,4},{6,7},{7,6},{8,9},{9,8},{10,11... | collective-permute-start | bytes 294920 | tf_op jit(solution)/shard_map/ppermute | solution.py:352
  17.9 0.0 collective-permute-done.7.refs_0_
  17.9 0.2 collective-permute-done.8.refs_1_
  18.1 0.2 collective-permute-done.3.refs_4_.refs_0_
  18.3 0.3 %collective-permute-done.4.refs_5_.refs_1_ = bf16[64,384]{1,0:T(8,128)(2,1)S(1)} collective-permute-done((bf16[64,384]{1,0:T(8,128)(2,1)S(1)}, bf16[64,384]{1,0:T(8,128)(2,1)S(1)}, u32[]{:S(2)}, u32[]{:S(2)}) %collective-permute-start.4) | collective-permute-done | bytes 49184 | tf_op jit(solution)/shard_map/ppermute | solution.py:340
  18.6 0.0 copy-done
  18.6 3.5 %shard_map.78.refs_6_ = bf16[4,8,6144]{2,1,0:T(8,128)(2,1)} custom-call(bf16[64,384]{1,0:T(8,128)(2,1)S(1)} %collective-permute-done.7.refs_0_, bf16[64,384]{1,0:T(8,128)(2,1)S(1)} %collective-permute-done.8.refs_1_, bf16[64,384]{1,0:T(8,128)(2,1)S(1)} %get-tuple-element.52.refs_2_, bf16[64,384]{1,0:T(8,128)(2,1)S(1)} %get-tuple-element.53.refs_3_, ...), custom_call_target="tpu_custom_call" | custom-call | flops 10000000000 | bytes 10000000 | tf_op jit(solution)/shard_map/pallas_call | solution.py:363
  22.1 0.0 collective-permute-done.6.refs_4_
  22.1 0.1 shard_map.79
  (2 shorter events, 0.0 us)
Async XLA Ops:
  2.2 4.9 %collective-permute-start.2 = (bf16[4,8,64,128]{3,2,1,0:T(8,128)(2,1)S(1)}, bf16[4,8,64,128]{3,2,1,0:T(8,128)(2,1)S(1)}, u32[]{:S(2)}, u32[]{:S(2)}) collective-permute-start(bf16[4,8,64,128]{3,2,1,0:T(8,128)(2,1)S(1)} %get-tuple-element.36.refs_0_), channel_id=1, source_target_pairs={{0,1},{1,0},{2,3},{3,2},{4,5},{5,4},{6,7},{7,6},{8,9},{9,8},{10,11... | collective-permute-start | bytes 1572872 | tf_op jit(solution)/shard_map/ppermute | solution.py:301
  5.5 10.4 %collective-permute-start = (bf16[2,64,384]{2,1,0:T(8,128)(2,1)S(1)}, bf16[2,64,384]{2,1,0:T(8,128)(2,1)S(1)}, u32[]{:S(2)}, u32[]{:S(2)}) collective-permute-start(bf16[2,64,384]{2,1,0:T(8,128)(2,1)S(1)} %get-tuple-element.34), channel_id=1, source_target_pairs={{0,2},{2,4},{4,6},{6,8},{8,10},{10,12},{12,14},{14,16},{16,18},{18... | collective-permute-start | bytes 294920 | tf_op jit(solution)/shard_map/ppermute | solution.py:299
  5.5 10.4 %collective-permute-start.1 = (bf16[2,64,384]{2,1,0:T(8,128)(2,1)S(1)}, bf16[2,64,384]{2,1,0:T(8,128)(2,1)S(1)}, u32[]{:S(2)}, u32[]{:S(2)}) collective-permute-start(bf16[2,64,384]{2,1,0:T(8,128)(2,1)S(1)} %get-tuple-element.35), channel_id=1, source_target_pairs={{0,2},{2,0},{4,6},{6,4},{8,10},{10,8},{12,14},{14,12},{16,18},{18,... | collective-permute-start | bytes 294920 | tf_op jit(solution)/shard_map/ppermute | solution.py:300
  14.4 3.1 %collective-permute-start.5 = (bf16[2,64,384]{2,1,0:T(8,128)(2,1)S(1)}, bf16[2,64,384]{2,1,0:T(8,128)(2,1)S(1)}, u32[]{:S(2)}, u32[]{:S(2)}) collective-permute-start(bf16[2,64,384]{2,1,0:T(8,128)(2,1)S(1)} %get-tuple-element.51), channel_id=1, source_target_pairs={{4,2},{8,6},{12,10},{16,14},{20,18},{24,22},{28,26},{32,30},{36,34... | collective-permute-start | bytes 294920 | tf_op jit(solution)/shard_map/ppermute | solution.py:321
  15.9 2.0 %collective-permute-start.7 = (bf16[64,384]{1,0:T(8,128)(2,1)S(1)}, bf16[64,384]{1,0:T(8,128)(2,1)S(1)}, u32[]{:S(2)}, u32[]{:S(2)}) collective-permute-start(bf16[64,384]{1,0:T(8,128)(2,1)S(1)} %get-tuple-element.52.refs_2_), channel_id=1, source_target_pairs={{0,1},{1,0},{2,3},{3,2},{4,5},{5,4},{6,7},{7,6},{8,9},{9,8},{10,11... | collective-permute-start | bytes 147464 | tf_op jit(solution)/shard_map/ppermute | solution.py:340
  16.9 1.2 %collective-permute-start.8 = (bf16[64,384]{1,0:T(8,128)(2,1)S(1)}, bf16[64,384]{1,0:T(8,128)(2,1)S(1)}, u32[]{:S(2)}, u32[]{:S(2)}) collective-permute-start(bf16[64,384]{1,0:T(8,128)(2,1)S(1)} %get-tuple-element.53.refs_3_), channel_id=1, source_target_pairs={{0,1},{1,0},{2,3},{3,2},{4,5},{5,4},{6,7},{7,6},{8,9},{9,8},{10,11... | collective-permute-start | bytes 147464 | tf_op jit(solution)/shard_map/ppermute | solution.py:340
  17.0 1.3 %collective-permute-start.3 = (bf16[64,384]{1,0:T(8,128)(2,1)S(1)}, bf16[64,384]{1,0:T(8,128)(2,1)S(1)}, u32[]{:S(2)}, u32[]{:S(2)}) collective-permute-start(bf16[64,384]{1,0:T(8,128)(2,1)S(1)} %get-tuple-element.49.refs_6_.refs_2_), channel_id=1, source_target_pairs={{0,1},{1,0},{2,3},{3,2},{4,5},{5,4},{6,7},{7,6},{8,9},{9,8},{10,11... | collective-permute-start | bytes 147464 | tf_op jit(solution)/shard_map/ppermute | solution.py:340
  17.4 1.2 %collective-permute-start.4 = (bf16[64,384]{1,0:T(8,128)(2,1)S(1)}, bf16[64,384]{1,0:T(8,128)(2,1)S(1)}, u32[]{:S(2)}, u32[]{:S(2)}) collective-permute-start(bf16[64,384]{1,0:T(8,128)(2,1)S(1)} %get-tuple-element.50.refs_7_.refs_3_), channel_id=1, source_target_pairs={{0,1},{1,0},{2,3},{3,2},{4,5},{5,4},{6,7},{7,6},{8,9},{9,8},{10,11... | collective-permute-start | bytes 147464 | tf_op jit(solution)/shard_map/ppermute | solution.py:340
  17.5 1.1 %copy-start = (s32[1,2]{1,0:T(1,128)S(1)}, s32[1,2]{1,0:T(1,128)}, u32[]{:S(2)}) copy-start(s32[1,2]{1,0:T(1,128)} %refs_10_.2) | copy-start | bytes 28
  17.5 4.6 %collective-permute-start.6 = (bf16[2,64,384]{2,1,0:T(8,128)(2,1)S(1)}, bf16[2,64,384]{2,1,0:T(8,128)(2,1)S(1)}, u32[]{:S(2)}, u32[]{:S(2)}) collective-permute-start(bf16[2,64,384]{2,1,0:T(8,128)(2,1)S(1)} %collective-permute-done.5.refs_5_), channel_id=1, source_target_pairs={{0,1},{1,0},{2,3},{3,2},{4,5},{5,4},{6,7},{7,6},{8,9},{9,8},{10,11... | collective-permute-start | bytes 294920 | tf_op jit(solution)/shard_map/ppermute | solution.py:352

commit v6 on v5

--- a/solution.py
+++ b/solution.py
@@ -192,12 +192,13 @@
 def early_kernel(*refs):
     packed1, packed2, part1, x1, x2, part2, inner = refs[8:]
 
-    @pl.when(is_corner())
+    @pl.when(jnp.logical_and(is_corner(), jnp.logical_not(is_first())))
     def _():
         first_body(*refs[:6], packed1, packed2, part1, x1, x2)
 
     @pl.when(is_first())
     def _():
+        first_body(*refs[:6], packed1, packed2, part1, x1, x2)
         middle_body(refs[3], refs[5], packed1, part1, x1, x2)
         second_body(x2, packed2, part2, inner)
 
@@ -294,7 +295,7 @@
         scratch_shapes=[VM((1, C), F32), VM((4, 8 * STEP, L), F32), DMA((8,))],
         compiler_params=PARAMS,
     )(clip, gain1, weight1, gain2, weight2)
-    turn = tiles - FAR // 2
+    turn = tiles - FAR + CORNER
     ups = {i: i + 1 for i in range(tiles)} | {turn: 0, tiles - 1: turn + 1}
     above = lax.ppermute(bottom, "tile", list(ups.items()))
     near = lax.ppermute(near, "tile", near_pairs)

time: 22.5 us -> 22.3 us (level)
  the two profiles are of different devices: /device:TPU:1 before, /device:TPU:7 now
where the time goes in v6:
time: 22.3 us; the launch traced here: 22.2 us
  Pallas kernels  12.6 us (57%)
  starting transfers between devices  8.66 us (39%)
  between operations  0.92 us (4%)
    pallas_call x1, Pallas kernels, local(): pl.pallas_call(early_kernel, out_shape=(edge, *state), in_specs=specs + [...  6.64 us
    pallas_call x1, Pallas kernels, local(): pl.pallas_call(even_kernel, out_shape=out, in_specs=[vmem] * 8 + specs, o...  3.47 us
    ppermute x1, starting transfers between devices, local(): other = lax.ppermute(top, 'tile', odd_pairs)  2.46 us
    pallas_call x1, Pallas kernels, local(): pl.pallas_call(send_kernel, out_shape=(VM((4, 8, BW * C), BF), VM((4, 8,...  2.21 us
    ppermute x4, starting transfers between devices, local(): early_halves = [lax.ppermute(x, 'tm', cores) for x in halves]  1.61 us
    ppermute x1, starting transfers between devices, local(): above = lax.ppermute(bottom, 'tile', list(ups.items()))  1.31 us
    ppermute x1, starting transfers between devices, local(): near = lax.ppermute(near, 'tile', near_pairs)  1.3 us
    ppermute x1, starting transfers between devices, local(): early_other = lax.ppermute(other, 'tm', cores)  1.22 us
  transfers between devices with their start and end apart: 9, of which 0 were waited for; matrix products, arithmetic and copies ran while one was open for 0% of the time, Pallas kernels for 47%

profile of v6, /device:TPU:7, one launch (start us, length us, event | category | flops | bytes accessed | tf_op | source)
XLA Modules:
  0.0 22.2 jit_solution(5386816284140515656)
XLA Ops:
  0.0 2.2 %shard_map.73 = (bf16[4,8,6144]{2,1,0:T(8,128)(2,1)S(1)}, bf16[4,8,64,128]{3,2,1,0:T(8,128)(2,1)S(1)}, bf16[2,64,384]{2,1,0:T(8,128)(2,1)S(1)}, bf16[2,64,384]{2...) custom-call(bf16[4,8,6144]{2,1,0:T(8,128)(2,1)} %clip_hbm.1, ...), custom_call_target="tpu_custom_call" | custom-call | tf_op jit(solution)/shard_map/pallas_call | solution.py:288
  2.2 0.8 %collective-permute-start.2 = (bf16[4,8,64,128]{3,2,1,0:T(8,128)(2,1)S(1)}, bf16[4,8,64,128]{3,2,1,0:T(8,128)(2,1)S(1)}, u32[]{:S(2)}, u32[]{:S(2)}) collective-permute-start(bf16[4,8,64,128]{3,2,1,0:T(8,128)(2,1)S(1)} %get-tuple-element.36.refs_0_), channel_id=1, source_target_pairs={{0,1},{1,0},{2,3},{3,2},{4,5},{5,4},{6,7},{7,6},{8,9},{9,8},{10,11... | collective-permute-start | bytes 1572872 | tf_op jit(solution)/shard_map/ppermute | solution.py:302
  3.0 1.3 %collective-permute-start = (bf16[2,64,384]{2,1,0:T(8,128)(2,1)S(1)}, bf16[2,64,384]{2,1,0:T(8,128)(2,1)S(1)}, u32[]{:S(2)}, u32[]{:S(2)}) collective-permute-start(bf16[2,64,384]{2,1,0:T(8,128)(2,1)S(1)} %get-tuple-element.34), channel_id=1, source_target_pairs={{0,2},{2,4},{4,6},{6,8},{8,10},{10,12},{12,14},{14,16},{16,18},{18... | collective-permute-start | bytes 294920 | tf_op jit(solution)/shard_map/ppermute | solution.py:300
  4.3 1.3 %collective-permute-start.1 = (bf16[2,64,384]{2,1,0:T(8,128)(2,1)S(1)}, bf16[2,64,384]{2,1,0:T(8,128)(2,1)S(1)}, u32[]{:S(2)}, u32[]{:S(2)}) collective-permute-start(bf16[2,64,384]{2,1,0:T(8,128)(2,1)S(1)} %get-tuple-element.35), channel_id=1, source_target_pairs={{0,2},{2,0},{4,6},{6,4},{8,10},{10,8},{12,14},{14,12},{16,18},{18,... | collective-permute-start | bytes 294920 | tf_op jit(solution)/shard_map/ppermute | solution.py:301
  6.2 0.0 collective-permute-done.2.refs_1_
  6.3 6.6 %shard_map.74 = (bf16[2,64,384]{2,1,0:T(8,128)(2,1)S(1)}, bf16[2,2304,256]{2,1,0:T(8,128)(2,1)S(1)}, bf16[2,2304,256]{2,1,0:T(8,128)(2,1)S(1)}, f32[2,384,256]{2...) custom-call(bf16[4,8,64,128]{3,2,1,0:T(8,128)(2,1)S(1)} %get-tuple-e, ...), custom_call_target="tpu_custom_call", output_to_operand_aliasing={{0}: (6, {})} | custom-call | tf_op jit(solution)/shard_map/pallas_call | solution.py:314
  12.9 2.5 %collective-permute-start.5 = (bf16[2,64,384]{2,1,0:T(8,128)(2,1)S(1)}, bf16[2,64,384]{2,1,0:T(8,128)(2,1)S(1)}, u32[]{:S(2)}, u32[]{:S(2)}) collective-permute-start(bf16[2,64,384]{2,1,0:T(8,128)(2,1)S(1)} %get-tuple-element.51), channel_id=1, source_target_pairs={{4,2},{8,6},{12,10},{16,14},{20,18},{24,22},{28,26},{32,30},{36,34... | collective-permute-start | bytes 294920 | tf_op jit(solution)/shard_map/ppermute | solution.py:322
  15.4 0.2 shard_map.75
  15.6 0.0 collective-permute-done.above
  15.6 0.0 collective-permute-done.1.near
  15.6 1.0 %collective-permute-start.7 = (bf16[64,384]{1,0:T(8,128)(2,1)S(1)}, bf16[64,384]{1,0:T(8,128)(2,1)S(1)}, u32[]{:S(2)}, u32[]{:S(2)}) collective-permute-start(bf16[64,384]{1,0:T(8,128)(2,1)S(1)} %get-tuple-element.52.refs_2_), channel_id=1, source_target_pairs={{0,1},{1,0},{2,3},{3,2},{4,5},{5,4},{6,7},{7,6},{8,9},{9,8},{10,11... | collective-permute-start | bytes 147464 | tf_op jit(solution)/shard_map/ppermute | solution.py:341
  16.6 0.1 collective-permute-start.8
  16.7 0.4 %collective-permute-start.3 = (bf16[64,384]{1,0:T(8,128)(2,1)S(1)}, bf16[64,384]{1,0:T(8,128)(2,1)S(1)}, u32[]{:S(2)}, u32[]{:S(2)}) collective-permute-start(bf16[64,384]{1,0:T(8,128)(2,1)S(1)} %get-tuple-element.49.refs_6_.refs_2_), channel_id=1, source_target_pairs={{0,1},{1,0},{2,3},{3,2},{4,5},{5,4},{6,7},{7,6},{8,9},{9,8},{10,11... | collective-permute-start | bytes 147464 | tf_op jit(solution)/shard_map/ppermute | solution.py:341
  17.1 0.1 collective-permute-start.4
  17.2 0.0 copy-start
  17.3 0.0 collective-permute-done.5.refs_5_
  17.3 1.2 %collective-permute-start.6 = (bf16[2,64,384]{2,1,0:T(8,128)(2,1)S(1)}, bf16[2,64,384]{2,1,0:T(8,128)(2,1)S(1)}, u32[]{:S(2)}, u32[]{:S(2)}) collective-permute-start(bf16[2,64,384]{2,1,0:T(8,128)(2,1)S(1)} %collective-permute-done.5.refs_5_), channel_id=1, source_target_pairs={{0,1},{1,0},{2,3},{3,2},{4,5},{5,4},{6,7},{7,6},{8,9},{9,8},{10,11... | collective-permute-start | bytes 294920 | tf_op jit(solution)/shard_map/ppermute | solution.py:353
  18.5 0.0 collective-permute-done.7.refs_0_
  18.5 0.0 collective-permute-done.8.refs_1_
  18.5 0.0 collective-permute-done.3.refs_4_.refs_0_
  18.5 0.0 collective-permute-done.4.refs_5_.refs_1_
  18.5 0.0 copy-done
  18.5 3.5 %shard_map.78.refs_6_ = bf16[4,8,6144]{2,1,0:T(8,128)(2,1)} custom-call(bf16[64,384]{1,0:T(8,128)(2,1)S(1)} %collective-permute-done.7.refs_0_, bf16[64,384]{1,0:T(8,128)(2,1)S(1)} %collective-permute-done.8.refs_1_, bf16[64,384]{1,0:T(8,128)(2,1)S(1)} %get-tuple-element.52.refs_2_, bf16[64,384]{1,0:T(8,128)(2,1)S(1)} %get-tuple-element.53.refs_3_, ...), custom_call_target="tpu_custom_call" | custom-call | flops 10000000000 | bytes 10000000 | tf_op jit(solution)/shard_map/pallas_call | solution.py:364
  22.0 0.0 collective-permute-done.6.refs_4_
  22.0 0.1 shard_map.79
  (2 shorter events, 0.0 us)
Async XLA Ops:
  2.2 4.0 %collective-permute-start.2 = (bf16[4,8,64,128]{3,2,1,0:T(8,128)(2,1)S(1)}, bf16[4,8,64,128]{3,2,1,0:T(8,128)(2,1)S(1)}, u32[]{:S(2)}, u32[]{:S(2)}) collective-permute-start(bf16[4,8,64,128]{3,2,1,0:T(8,128)(2,1)S(1)} %get-tuple-element.36.refs_0_), channel_id=1, source_target_pairs={{0,1},{1,0},{2,3},{3,2},{4,5},{5,4},{6,7},{7,6},{8,9},{9,8},{10,11... | collective-permute-start | bytes 1572872 | tf_op jit(solution)/shard_map/ppermute | solution.py:302
  3.0 12.6 %collective-permute-start = (bf16[2,64,384]{2,1,0:T(8,128)(2,1)S(1)}, bf16[2,64,384]{2,1,0:T(8,128)(2,1)S(1)}, u32[]{:S(2)}, u32[]{:S(2)}) collective-permute-start(bf16[2,64,384]{2,1,0:T(8,128)(2,1)S(1)} %get-tuple-element.34), channel_id=1, source_target_pairs={{0,2},{2,4},{4,6},{6,8},{8,10},{10,12},{12,14},{14,16},{16,18},{18... | collective-permute-start | bytes 294920 | tf_op jit(solution)/shard_map/ppermute | solution.py:300
  4.3 11.3 %collective-permute-start.1 = (bf16[2,64,384]{2,1,0:T(8,128)(2,1)S(1)}, bf16[2,64,384]{2,1,0:T(8,128)(2,1)S(1)}, u32[]{:S(2)}, u32[]{:S(2)}) collective-permute-start(bf16[2,64,384]{2,1,0:T(8,128)(2,1)S(1)} %get-tuple-element.35), channel_id=1, source_target_pairs={{0,2},{2,0},{4,6},{6,4},{8,10},{10,8},{12,14},{14,12},{16,18},{18,... | collective-permute-start | bytes 294920 | tf_op jit(solution)/shard_map/ppermute | solution.py:301
  12.9 4.3 %collective-permute-start.5 = (bf16[2,64,384]{2,1,0:T(8,128)(2,1)S(1)}, bf16[2,64,384]{2,1,0:T(8,128)(2,1)S(1)}, u32[]{:S(2)}, u32[]{:S(2)}) collective-permute-start(bf16[2,64,384]{2,1,0:T(8,128)(2,1)S(1)} %get-tuple-element.51), channel_id=1, source_target_pairs={{4,2},{8,6},{12,10},{16,14},{20,18},{24,22},{28,26},{32,30},{36,34... | collective-permute-start | bytes 294920 | tf_op jit(solution)/shard_map/ppermute | solution.py:322
  15.6 2.8 %collective-permute-start.7 = (bf16[64,384]{1,0:T(8,128)(2,1)S(1)}, bf16[64,384]{1,0:T(8,128)(2,1)S(1)}, u32[]{:S(2)}, u32[]{:S(2)}) collective-permute-start(bf16[64,384]{1,0:T(8,128)(2,1)S(1)} %get-tuple-element.52.refs_2_), channel_id=1, source_target_pairs={{0,1},{1,0},{2,3},{3,2},{4,5},{5,4},{6,7},{7,6},{8,9},{9,8},{10,11... | collective-permute-start | bytes 147464 | tf_op jit(solution)/shard_map/ppermute | solution.py:341
  16.6 1.8 %collective-permute-start.8 = (bf16[64,384]{1,0:T(8,128)(2,1)S(1)}, bf16[64,384]{1,0:T(8,128)(2,1)S(1)}, u32[]{:S(2)}, u32[]{:S(2)}) collective-permute-start(bf16[64,384]{1,0:T(8,128)(2,1)S(1)} %get-tuple-element.53.refs_3_), channel_id=1, source_target_pairs={{0,1},{1,0},{2,3},{3,2},{4,5},{5,4},{6,7},{7,6},{8,9},{9,8},{10,11... | collective-permute-start | bytes 147464 | tf_op jit(solution)/shard_map/ppermute | solution.py:341
  16.7 1.7 %collective-permute-start.3 = (bf16[64,384]{1,0:T(8,128)(2,1)S(1)}, bf16[64,384]{1,0:T(8,128)(2,1)S(1)}, u32[]{:S(2)}, u32[]{:S(2)}) collective-permute-start(bf16[64,384]{1,0:T(8,128)(2,1)S(1)} %get-tuple-element.49.refs_6_.refs_2_), channel_id=1, source_target_pairs={{0,1},{1,0},{2,3},{3,2},{4,5},{5,4},{6,7},{7,6},{8,9},{9,8},{10,11... | collective-permute-start | bytes 147464 | tf_op jit(solution)/shard_map/ppermute | solution.py:341
  17.1 1.3 %collective-permute-start.4 = (bf16[64,384]{1,0:T(8,128)(2,1)S(1)}, bf16[64,384]{1,0:T(8,128)(2,1)S(1)}, u32[]{:S(2)}, u32[]{:S(2)}) collective-permute-start(bf16[64,384]{1,0:T(8,128)(2,1)S(1)} %get-tuple-element.50.refs_7_.refs_3_), channel_id=1, source_target_pairs={{0,1},{1,0},{2,3},{3,2},{4,5},{5,4},{6,7},{7,6},{8,9},{9,8},{10,11... | collective-permute-start | bytes 147464 | tf_op jit(solution)/shard_map/ppermute | solution.py:341
  17.2 1.3 %copy-start = (s32[1,2]{1,0:T(1,128)S(1)}, s32[1,2]{1,0:T(1,128)}, u32[]{:S(2)}) copy-start(s32[1,2]{1,0:T(1,128)} %refs_10_.2) | copy-start | bytes 28
  17.3 4.7 %collective-permute-start.6 = (bf16[2,64,384]{2,1,0:T(8,128)(2,1)S(1)}, bf16[2,64,384]{2,1,0:T(8,128)(2,1)S(1)}, u32[]{:S(2)}, u32[]{:S(2)}) collective-permute-start(bf16[2,64,384]{2,1,0:T(8,128)(2,1)S(1)} %collective-permute-done.5.refs_5_), channel_id=1, source_target_pairs={{0,1},{1,0},{2,3},{3,2},{4,5},{5,4},{6,7},{7,6},{8,9},{9,8},{10,11... | collective-permute-start | bytes 294920 | tf_op jit(solution)/shard_map/ppermute | solution.py:353
